TPU v7x, 256 devices: a whole 4x4x8 slice. The times are simulated.
256 devices in a mesh: dp: 32 (over y, z), seq: 8 (over x, core).
Axes of the slice: x: 4, y: 4, z: 8, core: 2. Of those that a mesh axis runs over, the one named last changes fastest.
Arguments:
- qkvu: bfloat16 [32, 1024, 4096], P('dp', 'seq'), may hold values from -40 to 40
- lengths: int32 [32], P('dp'), may hold values from 128 to 1024, as said below
- items: bfloat16 [32, 8, 64, 2048], P('dp', 'seq'), may hold values from -6 to 6
- send_list: int32 [32, 8, 32, 2], P('dp', 'seq'), may hold values from 0 to 63
- send_count: int32 [32, 8, 32], P('dp', 'seq'), may hold values from 0 to 2, as said below
- w_out: bfloat16 [1024, 1024], replicated, may hold values from -0.1875 to 0.1875
- gain: float32 [1024], replicated, may hold values from 0.1 to 1.9
- g_hist: bfloat16 [32, 1024, 1024], P('dp', 'seq'), may hold values from -6 to 6
- g_tgt: bfloat16 [32, 8, 32, 2, 1024], P('dp', 'seq'), may hold values from -6 to 6
Outputs:
- hist_out: bfloat16 [32, 1024, 1024], P('dp', 'seq')
- tgt_out: bfloat16 [32, 8, 32, 2, 1024], P('dp', 'seq')
- d_qkvu: bfloat16 [32, 1024, 4096], P('dp', 'seq')
- d_items: bfloat16 [32, 8, 64, 2048], P('dp', 'seq')
- d_w2: float32 [1024, 1024], P(('dp', 'seq'))
Inputs may be any that keep to these rules, and one draw needn't show every extreme that they name: `lengths`: some user fills all 1024 rows in every draw. `send_count`: in every draw some receiving dp index gets 2 rows from every sender.
All inputs are finite; a program needn't handle non-finite values.
Results may differ from a plain program's by a relative error of at most 0.015.
Values may be sent and summed in bfloat16 or wider, within the bound.
A program may use at most 128 MiB of HBM per device.

v0:
```python
import math

import jax
import jax.numpy as jnp
from jax import lax
from jax.sharding import PartitionSpec as P

HD = 64


def forward_tiles(queries, query_pos, query_live, keys, values, length):
    count, heads, depth = queries.shape
    span = keys.shape[0]
    query_step = math.gcd(count, 512)
    key_advance = math.gcd(span, 512)
    scale = depth ** (-0.5)

    def one_block(inputs):
        query_tile, pos_tile, live_tile = inputs

        def tile_sum(offset_begin, total):
            key_tile = lax.dynamic_slice_in_dim(keys, offset_begin, key_advance, 0)
            value_tile = lax.dynamic_slice_in_dim(values, offset_begin, key_advance, 0)
            key_pos = offset_begin + lax.iota(jnp.int32, key_advance)
            allowed = (
                (key_pos[None, :] <= pos_tile[:, None])
                & (key_pos[None, :] < length)
                & live_tile[:, None]
            )
            score = scale * jnp.einsum(
                "qhe,khe->hqk", query_tile, key_tile, preferred_element_type=jnp.float32
            )
            weight = jnp.where(allowed[None], score * jax.nn.sigmoid(score), 0.0).astype(
                jnp.bfloat16
            )
            return total + jnp.einsum(
                "hqk,khe->qhe", weight, value_tile, preferred_element_type=jnp.float32
            )

        def add_tile(index, total):
            offset_begin = (index * key_advance).astype(jnp.int32)
            return tile_sum(offset_begin, total)

        return lax.fori_loop(
            0, span // key_advance, add_tile, jnp.zeros((query_step, heads, depth), jnp.float32)
        )

    parts = (
        queries.reshape(count // query_step, query_step, heads, depth),
        query_pos.reshape(count // query_step, query_step),
        query_live.reshape(count // query_step, query_step),
    )
    return lax.map(one_block, parts).reshape(count, heads, depth)


def backward_tiles(queries, grads, query_pos, query_live, keys, values, length):
    count, heads, depth = queries.shape
    span = keys.shape[0]
    query_step = math.gcd(count, 512)
    key_advance = math.gcd(span, 512)
    scale = depth ** (-0.5)

    def query_round(index, carry):
        grad_query, grad_key, grad_value = carry

        def tile_terms(offset_begin, inner_loop):
            query_part, key_sums, value_sums = inner_loop
            key_tile = lax.dynamic_slice_in_dim(keys, offset_begin, key_advance, 0)
            value_tile = lax.dynamic_slice_in_dim(values, offset_begin, key_advance, 0)
            key_pos = offset_begin + lax.iota(jnp.int32, key_advance)
            allowed = (
                (key_pos[None, :] <= query_pos[:, None])
                & (key_pos[None, :] < length)
                & query_live[:, None]
            )
            score = scale * jnp.einsum(
                "qhe,khe->hqk", queries, key_tile, preferred_element_type=jnp.float32
            )
            sigma = jax.nn.sigmoid(score)
            weight = jnp.where(allowed[None], score * sigma, 0.0).astype(jnp.bfloat16)
            d_weight = jnp.einsum(
                "qhe,khe->hqk", grads, value_tile, preferred_element_type=jnp.float32
            )
            d_score = jnp.where(
                allowed[None], d_weight * sigma * (1.0 + score * (1.0 - sigma)), 0.0
            ).astype(jnp.bfloat16)
            query_part = query_part + scale * jnp.einsum(
                "hqk,khe->qhe", d_score, key_tile, preferred_element_type=jnp.float32
            )
            key_term = scale * jnp.einsum(
                "hqk,qhe->khe", d_score, queries, preferred_element_type=jnp.float32
            )
            value_term = jnp.einsum(
                "hqk,qhe->khe", weight, grads, preferred_element_type=jnp.float32
            )
            key_sums = lax.dynamic_update_slice_in_dim(
                key_sums,
                lax.dynamic_slice_in_dim(key_sums, offset_begin, key_advance, 0) + key_term,
                offset_begin,
                0,
            )
            value_sums = lax.dynamic_update_slice_in_dim(
                value_sums,
                lax.dynamic_slice_in_dim(value_sums, offset_begin, key_advance, 0) + value_term,
                offset_begin,
                0,
            )
            return (query_part, key_sums, value_sums)

        def key_cycle(key_index, inner_loop):
            offset_begin = (key_index * key_advance).astype(jnp.int32)
            return tile_terms(offset_begin, inner_loop)

        start_carry = (jnp.zeros((query_step, heads, depth), jnp.float32), grad_key, grad_value)
        query_part, grad_key, grad_value = lax.fori_loop(
            0, span // key_advance, key_cycle, start_carry
        )
        grad_query = query_part
        return (grad_query, grad_key, grad_value)

    zeros_query = jnp.zeros((count, heads, depth), jnp.float32)
    zeros_key = jnp.zeros((span, heads, depth), jnp.float32)
    return lax.fori_loop(0, count // query_step, query_round, (zeros_query, zeros_key, zeros_key))


def norm_rows(attended, gain, gate):
    values = attended.astype(jnp.float32)
    centred = values - jnp.mean(values, axis=1, keepdims=True)
    inverse = lax.rsqrt(jnp.mean(centred * centred, axis=1, keepdims=True) + 1e-05)
    norm_result = centred * inverse
    gated = (norm_result * gain[None, :] * gate.astype(jnp.float32)).astype(jnp.bfloat16)
    return (gated, norm_result, inverse)


def norm_back(d_gated, norm_result, inverse, gain, gate):
    scaled = d_gated * gain[None, :]
    d_gate = (scaled * norm_result).astype(jnp.bfloat16)
    d_norm = scaled * gate.astype(jnp.float32)
    d_att = inverse * (
        d_norm
        - jnp.mean(d_norm, axis=1, keepdims=True)
        - norm_result * jnp.mean(d_norm * norm_result, axis=1, keepdims=True)
    )
    return (d_gate, d_att.astype(jnp.bfloat16))


def shards(qkvu, lengths, items, send_list, send_count, w_out, gain, g_hist, g_tgt):
    width = gain.shape[0]
    heads = width // HD
    count = qkvu.shape[1]
    seats = lax.axis_size("seq")
    groups = lax.axis_size("dp")
    length = lengths[0]
    lists = send_list[0, 0]
    slot_count = lists.shape[1]
    slot_live = lax.broadcasted_iota(jnp.int32, lists.shape, 1) < send_count[0, 0][:, None]
    picked = jnp.take(items[0, 0], lists, axis=0)
    picked = jnp.where(slot_live[:, :, None], picked, jnp.zeros_like(picked))
    arrived = lax.all_to_all(picked, "dp", split_axis=0, concat_axis=0, tiled=True)
    targets = arrived.reshape(groups * slot_count, 2 * width)
    slots = targets.shape[0]
    target_query = targets[:, :width]
    target_gate = targets[:, width:]
    history = qkvu[0]
    gate = history[:, :width]
    queries = history[:, 2 * width : 3 * width].reshape(count, heads, HD)
    keys_all, values_all = (
        lax.all_gather(history[:, 3 * width :], "seq", axis=0, tiled=True),
        lax.all_gather(history[:, width : 2 * width], "seq", axis=0, tiled=True),
    )
    span = keys_all.shape[0]
    keys = keys_all.reshape(span, heads, HD)
    values = values_all.reshape(span, heads, HD)
    tq_heads = target_query.reshape(slots, heads, HD)
    hist_pos = lax.axis_index("seq") * count + lax.iota(jnp.int32, count)
    hist_live = hist_pos < length
    target_pos = jnp.full((slots,), span, jnp.int32)
    target_live = jnp.ones((slots,), bool)
    att_hist = (
        forward_tiles(queries, hist_pos, hist_live, keys, values, length)
        .astype(jnp.bfloat16)
        .reshape(count, width)
    )
    att_tgt = (
        forward_tiles(tq_heads, target_pos, target_live, keys, values, length)
        .astype(jnp.bfloat16)
        .reshape(slots, width)
    )
    history_gated, normed_hist, inverse_hist = norm_rows(att_hist, gain, gate)
    gated_tgt, normed_tgt, inverse_tgt = norm_rows(att_tgt, gain, target_gate)
    gated_all = jnp.concatenate([history_gated, gated_tgt], axis=0)
    cot_all = jnp.concatenate([g_hist[0], g_tgt[0, 0].reshape(slots, width)], axis=0)
    outputs = jnp.dot(gated_all, w_out, preferred_element_type=jnp.float32).astype(jnp.bfloat16)
    d_gated = lax.dot_general(
        cot_all, w_out, (((1,), (1,)), ((), ())), preferred_element_type=jnp.float32
    )
    du_hist, datt_hist = norm_back(d_gated[:count], normed_hist, inverse_hist, gain, gate)
    du_tgt, datt_tgt = norm_back(d_gated[count:], normed_tgt, inverse_tgt, gain, target_gate)
    weight_sums = lax.psum_scatter(
        lax.dot_general(
            gated_all, cot_all, (((0,), (0,)), ((), ())), preferred_element_type=jnp.float32
        ),
        ("dp", "seq"),
        scatter_dimension=0,
        tiled=True,
    )
    d_w2 = weight_sums * (groups * count * seats) ** (-0.5)
    gq_hist, gk_hist, gv_hist = backward_tiles(
        queries, datt_hist.reshape(count, heads, HD), hist_pos, hist_live, keys, values, length
    )
    gq_tgt, gk_tgt, gv_tgt = backward_tiles(
        tq_heads, datt_tgt.reshape(slots, heads, HD), target_pos, target_live, keys, values, length
    )
    key_terms = jnp.stack(
        [(gv_hist + gv_tgt).reshape(span, width), (gk_hist + gk_tgt).reshape(span, width)], axis=1
    )
    summed = lax.psum_scatter(key_terms, "seq", scatter_dimension=0, tiled=True).astype(
        jnp.bfloat16
    )
    d_attn = jnp.concatenate(
        [summed[:, 0], gq_hist.astype(jnp.bfloat16).reshape(count, width), summed[:, 1]], axis=1
    )
    dq_targets = gq_tgt.astype(jnp.bfloat16).reshape(slots, width)
    d_qkvu = jnp.concatenate([du_hist, d_attn], axis=1)
    sent_back = jnp.concatenate([dq_targets, du_tgt], axis=1).reshape(groups, slot_count, 2 * width)
    returned = lax.all_to_all(sent_back, "dp", split_axis=0, concat_axis=0, tiled=True)
    item_count = items.shape[2]
    table = (
        lists[:, :, None] == lax.broadcasted_iota(jnp.int32, (1, 1, item_count), 2)
    ) & slot_live[:, :, None]
    d_items = jnp.einsum(
        "gcr,gcf->rf", table.astype(jnp.bfloat16), returned, preferred_element_type=jnp.float32
    ).astype(jnp.bfloat16)
    hist_out = outputs[:count]
    tgt_out = outputs[count:].reshape(1, 1, groups, slot_count, width)
    return (hist_out[None], tgt_out, d_qkvu[None], d_items[None, None], d_w2)


def solution(mesh):
    in_specs = (
        P("dp", "seq", None),
        P("dp"),
        P("dp", "seq", None, None),
        P("dp", "seq", None, None),
        P("dp", "seq", None),
        P(),
        P(),
        P("dp", "seq", None),
        P("dp", "seq", None, None, None),
    )
    out_specs = (
        P("dp", "seq", None),
        P("dp", "seq", None, None, None),
        P("dp", "seq", None),
        P("dp", "seq", None, None),
        P(("dp", "seq"), None),
    )
    return jax.shard_map(shards, mesh=mesh, in_specs=in_specs, out_specs=out_specs, check_vma=False)
```

profile of v0, /device:TPU:1, one launch (start us, length us, event | category | flops | bytes accessed | tf_op | source)
XLA Modules:
  0.0 450.9 jit_solution(6153633876517975480)
XLA Ops:
  13.2 12.0 %all-to-all-start = ((bf16[32,2,2048]{2,1,0:T(2,128)(2,1)}), bf16[32,2,2048]{2,1,0:T(2,128)(2,1)S(1)}, u32[]{:S(2)}, u32[]{:S(2)}) async-start(bf16[32,2,2048]{2,1,0:T(2,128)(2,1)} %broadcast_select_fusion.1), calls=%async_computation | async-start | bytes 524288 | tf_op jit(solution)/shard_map/all_to_all | solution.py:159
  28.3 6.6 %all-to-all-done = bf16[32,2,2048]{2,1,0:T(2,128)(2,1)S(1)} async-done(((bf16[32,2,2048]{2,1,0:T(2,128)(2,1)}), bf16[32,2,2048]{2,1,0:T(2,128)(2,1)S(1)}, u32[]{:S(2)}, u32[]{:S(2)}) %all-to-all-start) | async-done | bytes 262176 | tf_op jit(solution)/shard_map/all_to_all | solution.py:159
  37.6 4.8 %all-gather.5.cloned.1.call-done = bf16[1024,1024]{1,0:T(8,128)(2,1)} async-done(((bf16[128,1024]{1,0:T(8,128)(2,1)}), bf16[1024,1024]{1,0:T(8,128)(2,1)}) %all-gather.5.cloned.1.call-update) | async-done | bytes 2097168 | tf_op jit(solution)/shard_map/all_gather | solution.py:168
  42.4 4.0 copy.74
  46.4 26.0 %all-gather.3.cloned.1.call-done = bf16[1024,1024]{1,0:T(8,128)(2,1)} async-done(((bf16[128,1024]{1,0:T(8,128)(2,1)}), bf16[1024,1024]{1,0:T(8,128)(2,1)}) %all-gather.3.cloned.1.call-update) | async-done | bytes 2097168 | tf_op jit(solution)/shard_map/all_gather | solution.py:169
  72.3 4.0 copy.73
  76.3 8.4 %while.104 = (s32[]{:T(128)}, f32[64,16,64]{0,2,1:T(8,128)}, bf16[1024,16,64]{0,2,1:T(8,128)(2,1)}, s32[]{:T(128)}, bf16[1024,16,64]{0,2,1:T(8,128)(2,1)}, /*ind...) while((s32[]{:T(128)}, f32[64,16,64]{0,2,1:T(8,128)}, ...), condition=%wide.region_5.6_spmd.clone, body=%wide.region_4.5_spmd.clone.sunk | while | flops 138020864 | bytes 3148460 | solution.py:44
  77.0 3.4 fusion.179
  81.1 3.6 fusion.179
  84.7 10.2 %while.106 = (s32[]{:T(128)}, f32[128,16,64]{0,2,1:T(8,128)S(1)}, bf16[1024,16,64]{0,2,1:T(8,128)(2,1)}, s32[]{:T(128)}, bf16[1024,16,64]{0,2,1:T(8,128)(2,1)}, ...) while((s32[]{:T(128)}, f32[128,16,64]{0,2,1:T(8,128)S(1)}, ...), condition=%wide.region_1.2_spmd.clone.clone.clone, body=%wide.region_0.1_spmd.clone.clone.clone.sunk | while | flops 276236160 | bytes 3547076 | solution.py:44
  86.3 3.5 fusion.199
  91.4 3.5 fusion.199
  113.5 3.6 fusion.107
  122.2 29.1 %while.107 = (s32[]{:T(128)}, f32[128,16,64]{0,2,1:T(8,128)S(1)}, f32[1024,16,64]{0,2,1:T(8,128)}, f32[1024,16,64]{0,2,1:T(8,128)}, bf16[1024,16,64]{0,2,1:T(8,1...) while((s32[]{:T(128)}, f32[128,16,64]{0,2,1:T(8,128)S(1)}, ...), condition=%wide.region_11.12_spmd.clone.clone.clone, body=%wide.region_10.11_spmd.clone.clone.clone.sunk | while | flops 692127616 | bytes 116595360 | solution.py:115
  156.4 23.4 %while.105 = (s32[]{:T(128)}, f32[64,16,64]{0,2,1:T(8,128)S(1)}, f32[1024,16,64]{0,2,1:T(8,128)}, f32[1024,16,64]{0,2,1:T(8,128)}, bf16[1024,16,64]{0,2,1:T(8,12...) while((s32[]{:T(128)}, f32[64,16,64]{0,2,1:T(8,128)S(1)}, ...), condition=%wide.region_15.16_spmd.clone, body=%wide.region_14.15_spmd.clone.sunk | while | flops 346753024 | bytes 107087768 | solution.py:115
  179.7 6.8 %add.368 = f32[1024,16,64]{0,2,1:T(8,128)} add(f32[1024,16,64]{0,2,1:T(8,128)} %get-tuple-element.765, f32[1024,16,64]{0,2,1:T(8,128)} %get-tuple-element.766) | non-fusion elementwise | flops 1048576 | bytes 12582912 | tf_op jit(solution)/shard_map/add | solution.py:215
  186.5 5.4 %copy.86 = f32[1024,1,1024]{2,0,1:T(8,128)} copy(f32[1024,1,1024]{0,2,1:T(8,128)} %bitcast.249) | data formatting | bytes 8388608 | tf_op jit(solution)/shard_map/stack;reshape | solution.py:214
  191.9 6.8 %add.367 = f32[1024,16,64]{0,2,1:T(8,128)} add(f32[1024,16,64]{0,2,1:T(8,128)} %get-tuple-element.763, f32[1024,16,64]{0,2,1:T(8,128)} %get-tuple-element.764) | non-fusion elementwise | flops 1048576 | bytes 12582912 | tf_op jit(solution)/shard_map/add | solution.py:215
  198.7 5.5 %copy.85 = f32[1024,1,1024]{2,0,1:T(8,128)} copy(f32[1024,1,1024]{0,2,1:T(8,128)} %bitcast.250) | data formatting | bytes 8388608 | tf_op jit(solution)/shard_map/stack;reshape | solution.py:214
  204.2 8.4 %pad_maximum_fusion = f32[1024,2,1024]{2,0,1:T(8,128)} fusion(f32[1024,1,1024]{2,0,1:T(8,128)} %copy.86, f32[1024,1,1024]{2,0,1:T(8,128)} %copy.85), kind=kLoop, calls=%fused_computation.122 | loop fusion | flops 2097152 | bytes 16777216 | tf_op jit(solution)/shard_map/stack | solution.py:214
  218.4 9.6 %all-to-all-start.1 = ((bf16[32,2,2048]{2,1,0:T(2,128)(2,1)}), bf16[32,2,2048]{2,1,0:T(2,128)(2,1)S(1)}, u32[]{:S(2)}, u32[]{:S(2)}) async-start(bf16[32,2,2048]{2,1,0:T(2,128)(2,1)} %pad_maximum_fusion.3), calls=%async_computation.2 | async-start | bytes 524288 | tf_op jit(solution)/shard_map/all_to_all | solution.py:226
  232.7 5.4 %all-to-all-done.1 = bf16[32,2,2048]{2,1,0:T(2,128)(2,1)S(1)} async-done(((bf16[32,2,2048]{2,1,0:T(2,128)(2,1)}), bf16[32,2,2048]{2,1,0:T(2,128)(2,1)S(1)}, u32[]{:S(2)}, u32[]{:S(2)}) %all-to-all-start.1) | async-done | bytes 262176 | tf_op jit(solution)/shard_map/all_to_all | solution.py:226
  239.2 145.4 %all-reduce.3.cloned.1.call-done = f32[1024,1024]{1,0:T(8,128)} async-done(((f32[1024,1024]{1,0:T(8,128)}), f32[1024,1024]{1,0:T(8,128)}) %all-reduce.3.cloned.1.call-update) | async-done | bytes 4194320
  386.0 55.9 %reduce-scatter.2.cloned.1.call-done = f32[128,2,1024]{2,0,1:T(8,128)} async-done(((f32[1024,2,1024]{2,0,1:T(8,128)}), f32[128,2,1024]{2,0,1:T(8,128)}) %reduce-scatter.2.cloned.1.call-update) | async-done | bytes 1048592 | tf_op jit(solution)/shard_map/reduce_scatter | solution.py:217
  (214 shorter events, 111.8 us)
Async XLA Ops:
  7.2 19.4 %copy-start = (bf16[1024,1024]{1,0:T(8,128)(2,1)S(1)}, bf16[1024,1024]{1,0:T(8,128)(2,1)}, u32[]{:S(2)}) copy-start(bf16[1024,1024]{1,0:T(8,128)(2,1)} %param.22) | copy-start | bytes 6291460
  7.2 3.1 copy-start.36
  7.2 3.9 copy-start.13
  7.2 35.2 %all-gather.5.cloned.1.call-start = ((), (), s32[]{:S(2)}) async-start(), calls=%async_computation.4 | async-start | bytes 2359296 | tf_op jit(solution)/shard_map/all_gather | solution.py:168
  9.4 62.9 %all-gather.3.cloned.1.call-start = ((), (), s32[]{:S(2)}) async-start(), calls=%async_computation.3 | async-start | bytes 2359296 | tf_op jit(solution)/shard_map/all_gather | solution.py:169
  9.5 15.8 %copy-start.30 = (bf16[1,1,32,2,1024]{4,3,2,1,0:T(2,128)(2,1)S(1)}, bf16[1,1,32,2,1024]{4,3,2,1,0:T(2,128)(2,1)}, u32[]{:S(2)}) copy-start(bf16[1,1,32,2,1024]{4,3,2,1,0:T(2,128)(2,1)} %param.25) | copy-start | bytes 393220
  11.1 15.5 %copy-start.20 = (bf16[1,128,1024]{2,1,0:T(8,128)(2,1)S(1)}, bf16[1,128,1024]{2,1,0:T(8,128)(2,1)}, u32[]{:S(2)}) copy-start(bf16[1,128,1024]{2,1,0:T(8,128)(2,1)} %param.24) | copy-start | bytes 786436
  13.2 21.7 %all-to-all-start = ((bf16[32,2,2048]{2,1,0:T(2,128)(2,1)}), bf16[32,2,2048]{2,1,0:T(2,128)(2,1)S(1)}, u32[]{:S(2)}, u32[]{:S(2)}) async-start(bf16[32,2,2048]{2,1,0:T(2,128)(2,1)} %broadcast_select_fusion.1), calls=%async_computation | async-start | bytes 524288 | tf_op jit(solution)/shard_map/all_to_all | solution.py:159
  25.2 359.4 %all-reduce.3.cloned.1.call-start = ((), (), s32[]{:S(2)}) async-start(), calls=%async_computation.6 | async-start | bytes 8388608
  76.3 8.4 %copy-start.14 = (f32[128,16,64]{0,2,1:T(8,128)S(1)}, f32[128,16,64]{0,2,1:T(8,128)}, u32[]{:S(2)}) copy-start(f32[128,16,64]{0,2,1:T(8,128)} %custom-call) | copy-start | bytes 1572868
  96.3 6.5 %copy-start.31 = (f32[1024]{0:T(1024)S(1)}, f32[1024]{0:T(1024)}, u32[]{:S(2)}) copy-start(f32[1024]{0:T(1024)} %param.23) | copy-start | bytes 12292
  104.2 9.3 %copy-start.19 = (bf16[64,1024]{1,0:T(8,128)(2,1)S(1)}, bf16[64,1024]{1,0:T(8,128)(2,1)}, u32[]{:S(2)}) copy-start(bf16[64,1024]{1,0:T(8,128)(2,1)} %copy-done.18) | copy-start | bytes 393220
  106.5 7.0 %copy-start.21 = (bf16[1,128,1024]{2,1,0:T(8,128)(2,1)S(1)}, bf16[1,128,1024]{2,1,0:T(8,128)(2,1)}, u32[]{:S(2)}) copy-start(bf16[1,128,1024]{2,1,0:T(8,128)(2,1)} %param.24) | copy-start | bytes 786436
  106.5 7.0 %copy-start.22 = (bf16[128,1024]{1,0:T(8,128)(2,1)S(1)}, bf16[128,1024]{1,0:T(8,128)(2,1)}, u32[]{:S(2)}) copy-start(bf16[128,1024]{1,0:T(8,128)(2,1)} %get-tuple-element.1130) | copy-start | bytes 786436
  117.1 324.8 %reduce-scatter.2.cloned.1.call-start = ((), (), s32[]{:S(2)}) async-start(), calls=%async_computation.5 | async-start | bytes 9437184 | tf_op jit(solution)/shard_map/reduce_scatter | solution.py:217
  130.0 3.8 copy-start.5
  144.6 3.7 copy-start.5
  212.7 15.3 %copy-start.23 = (bf16[128,1024]{1,0:T(8,128)(2,1)S(1)}, bf16[128,1024]{1,0:T(8,128)(2,1)}, u32[]{:S(2)}) copy-start(bf16[128,1024]{1,0:T(8,128)(2,1)} %get-tuple-element.1130) | copy-start | bytes 786436
  212.7 15.3 %copy-start.26 = (bf16[64,1024]{1,0:T(8,128)(2,1)S(1)}, bf16[64,1024]{1,0:T(8,128)(2,1)}, u32[]{:S(2)}) copy-start(bf16[64,1024]{1,0:T(8,128)(2,1)} %get-tuple-element.1137) | copy-start | bytes 393220
  218.4 19.7 %all-to-all-start.1 = ((bf16[32,2,2048]{2,1,0:T(2,128)(2,1)}), bf16[32,2,2048]{2,1,0:T(2,128)(2,1)S(1)}, u32[]{:S(2)}, u32[]{:S(2)}) async-start(bf16[32,2,2048]{2,1,0:T(2,128)(2,1)} %pad_maximum_fusion.3), calls=%async_computation.2 | async-start | bytes 524288 | tf_op jit(solution)/shard_map/all_to_all | solution.py:226
  228.0 10.1 %copy-start.33 = (s32[1,1,32,2]{2,3,1,0:T(2,128)S(1)}, s32[1,1,32,2]{2,3,1,0:T(2,128)}, u32[]{:S(2)}) copy-start(s32[1,1,32,2]{2,3,1,0:T(2,128)} %param.20) | copy-start | bytes 772
  228.0 10.1 %copy-start.35 = (pred[32,2]{0,1:T(4,128)(4,1)S(1)}, pred[32,2]{0,1:T(4,128)(4,1)}, u32[]{:S(2)}) copy-start(pred[32,2]{0,1:T(4,128)(4,1)} %copy-done.34) | copy-start | bytes 196
  230.1 213.1 %copy-start.24 = (bf16[128,1024]{1,0:T(8,128)(2,1)S(1)}, bf16[128,1024]{1,0:T(8,128)(2,1)}, u32[]{:S(2)}) copy-start(bf16[128,1024]{1,0:T(8,128)(2,1)} %get-tuple-element.1131) | copy-start | bytes 786436
  231.0 212.3 %copy-start.25 = (bf16[128,1024]{1,0:T(8,128)(2,1)S(1)}, bf16[128,1024]{1,0:T(8,128)(2,1)}, u32[]{:S(2)}) copy-start(bf16[128,1024]{1,0:T(8,128)(2,1)} %copy.87) | copy-start | bytes 786436
  (32 other events, 67.9 us)
Sparse Core Ops, SparseCore 0:
  10.5 31.8 all-gather.4
  44.3 28.0 all-gather.2
  117.2 267.3 all-reduce.2
  387.2 54.7 reduce-scatter.1
where the time goes:
time: 452 us; the launch traced here: 451 us
  waiting for transfers between devices  245 us (54%)
  local copies, waits for them, and re-layouts  72.3 us (16%)
  other arithmetic  50.3 us (11%)
  matrix products  46.9 us (10%)
  starting transfers between devices  21.8 us (5%)
  between operations  14.2 us (3%)
    unnamed x5, waiting for transfers between devices  146 us
    reduce_scatter x1, waiting for transfers between devices, shards(): lax.psum_scatter(key_terms, 'seq', scatter_dimension=0, tiled=True)  55.9 us
    all_gather x1, waiting for transfers between devices, shards(): lax.all_gather(history[:, width:2 * width], 'seq', axis=0, tiled=True)  26 us
    while x52, local copies, waits for them, and re-layouts  21.6 us
    dot_general x4, matrix products, tile_sum(): jnp.einsum('hqk,khe->qhe', weight, value_tile, preferred_element_type=jnp...  14.1 us
    all_to_all x1, starting transfers between devices, shards(): lax.all_to_all(picked, 'dp', split_axis=0, concat_axis=0, tiled=True)  12 us
    another operation x2, local copies, waits for them, and re-layouts, shards(): jnp.stack([(gv_hist + gv_tgt).reshape(span, width), (gk_hist + gk_tgt).re...  10.9 us
    another operation x4, local copies, waits for them, and re-layouts  10.1 us
  transfers between devices with their start and end apart: 6, of which 6 were waited for; matrix products, arithmetic and copies ran while one was open for 21% of the time, Pallas kernels for 0%

commit v1 on v0

v1 whole, which is shorter than its diff:
```python
import jax
import jax.numpy as jnp
from jax import lax
from jax.experimental import pallas as pl
from jax.experimental.pallas import tpu as pltpu
from jax.sharding import PartitionSpec as P

BF = jnp.bfloat16
F32 = jnp.float32
MESH = pl.DeviceIdType.MESH

D = 1024
SEQ = 8
DP = 32
NY = 4
NZ = 8
ROWS = 128
SLOTS = 64
HIST = 1024
ALL = 1536
TILE = 256
WIDE = 2 * TILE

(PK, PQ, PV, PT, PTQ, PAH, PAT, PDH, PDT, PGT, PQS, PQD, PGQ, PGK, PGV, PC, PY, PZ, PX, NPH) = range(20)
(LIN, LW, LCOT, LU, LHO, LTO, LDU, LGR, LDI, LDW, NLOC) = range(11)


def dot(a, b):
    return lax.dot_general(a, b, (((1,), (0,)), ((), ())), preferred_element_type=F32)


def dot_nt(a, b):
    return lax.dot_general(a, b, (((1,), (1,)), ((), ())), preferred_element_type=F32)


def dot_tn(a, b):
    return lax.dot_general(a, b, (((0,), (0,)), ((), ())), preferred_element_type=F32)


def one_hot(condition):
    return jnp.where(condition, 1.0, 0.0).astype(BF)


def kernel(
    code, length_ref, qkvu, items, w_hbm, gain, gh_hbm, gt_hbm,
    ho_out, to_out, dqkvu_out, di_out, dw_out,
    kraw, vraw, qraw, qs, kst, vst, wst, gst, dsc,
    u_v, w_v, cot, dz, sel_t, tsend, trecv, tq, tgate,
    o_h, att_r, datt, da_raw, da, gated, outs, du_h, dgt, zg, rg, dqt, yq, zq, rq,
    gq, gk, gv, di, p_send, p_own, c_recv, y_send, y_own, y_recv, z_send, z_own, z_recv, x_send, x_recv, dw,
    ssem, rsem, lsem,
):
    g = lax.axis_index("dp")
    s = lax.axis_index("seq")
    y, z = lax.div(g, NZ), lax.rem(g, NZ)
    core = lax.rem(s, 2)
    length = length_ref[0]

    def rows_at(index, size):
        return pl.ds(pl.multiple_of(index * size, size), size)

    barrier = pltpu.get_barrier_semaphore()

    def greet_dp(d, carry):
        pl.semaphore_signal(barrier, inc=1, device_id={"dp": lax.rem(g + d, DP)}, device_id_type=MESH)
        return carry

    for d in range(1, SEQ):
        pl.semaphore_signal(barrier, inc=1, device_id={"seq": lax.rem(s + d, SEQ)}, device_id_type=MESH)
    lax.fori_loop(1, DP, greet_dp, 0)

    def local(src, dst, sem):
        copy = pltpu.make_async_copy(src, dst, lsem.at[sem])
        copy.start()

    def local_wait(ref, sem):
        pltpu.make_async_copy(ref, ref, lsem.at[sem]).wait()

    def send(src, dst, phase, device):
        pltpu.make_async_remote_copy(
            src_ref=src, dst_ref=dst, send_sem=ssem.at[phase], recv_sem=rsem.at[phase],
            device_id=device, device_id_type=MESH,
        ).start()

    def seq_send(phase, src, dst):
        for d in range(1, SEQ):
            p = lax.rem(s + d, SEQ)
            send(src(p), dst, phase, {"seq": p})

    def got(ref, phase):
        pltpu.make_async_copy(ref, ref, rsem.at[phase]).wait()

    def sent(ref, phase):
        pltpu.make_async_copy(ref, ref, ssem.at[phase]).wait()

    for base, buf in ((3 * D, kraw), (2 * D, qraw), (D, vraw)):
        local(qkvu.at[:, pl.ds(pl.multiple_of(base + s * 128, 128), 128)], buf.at[rows_at(s, ROWS)], LIN)
    local(w_hbm, w_v, LW)
    local(gh_hbm, cot.at[pl.ds(0, ROWS)], LCOT)
    local(gt_hbm, cot.at[pl.ds(ROWS, SLOTS)], LCOT)
    local(qkvu.at[:, pl.ds(0, D)], u_v, LU)

    sel_t[...] = one_hot(lax.broadcasted_iota(jnp.int32, (512, 512), 0) == code[...])
    stacked = jnp.concatenate(
        [
            jnp.concatenate([items[:, 128 * k : 128 * k + 128], items[:, D + 128 * k : D + 128 * k + 128]], axis=1)
            for k in range(SEQ)
        ],
        axis=0,
    )
    tsend[...] = dot_tn(sel_t[...], stacked).astype(BF)

    pl.semaphore_wait(barrier, SEQ - 1 + DP - 1)

    def dp_send(phase, src, dst):
        def one(d, carry):
            p = lax.rem(g + d, DP)
            send(src.at[rows_at(p, 16)], dst.at[rows_at(g, 16)], phase, {"dp": p})
            return carry

        lax.fori_loop(1, DP, one, 0)

    for phase, base, buf in ((PK, 3 * D, kraw), (PQ, 2 * D, qraw), (PV, D, vraw)):
        seq_send(
            phase,
            lambda p, base=base: qkvu.at[:, pl.ds(pl.multiple_of(base + p * 128, 128), 128)],
            buf.at[rows_at(s, ROWS)],
        )
    dp_send(PT, tsend, trecv)
    trecv[rows_at(g, 16), :] = tsend[rows_at(g, 16), :]

    local_wait(w_v, LW)
    local_wait(cot, LCOT)
    local_wait(u_v, LU)
    dz[...] = dot_nt(cot[...], w_v[...])

    row512 = lax.broadcasted_iota(jnp.int32, (512, 512), 0)
    col512 = lax.broadcasted_iota(jnp.int32, (512, 512), 1)
    perm = one_hot(col512 == ((row512 & 63) >> 1) * 16 + (row512 >> 6) * 2 + (row512 & 1))
    perm_back = one_hot(row512 == ((col512 & 63) >> 1) * 16 + (col512 >> 6) * 2 + (col512 & 1))

    got(trecv.at[pl.ds(0, 496)], PT)
    arranged = dot(perm, trecv[...]).astype(BF)
    tq[...] = arranged[:, :128]
    for k in range(SEQ):
        tgate[:, 128 * k : 128 * k + 128] = arranged[64 * k : 64 * k + 64, 128:]
    target_rows = pl.ds(pl.multiple_of(HIST + s * SLOTS, SLOTS), SLOTS)
    seq_send(PTQ, lambda p: tq.at[rows_at(p, SLOTS)], qraw.at[target_rows])
    qraw[target_rows, :] = tq[rows_at(s, SLOTS), :]

    for buf in (kraw, qraw, vraw):
        local_wait(buf.at[pl.ds(0, ROWS)], LIN)
    lane = lax.broadcasted_iota(jnp.int32, (TILE, 128), 1)
    tile_row = lax.broadcasted_iota(jnp.int32, (TILE, 128), 0)

    def stack_heads(raw, out):
        for j in range(4):
            block = raw[TILE * j : TILE * j + TILE, :].astype(F32)
            live = tile_row < length - TILE * j
            out[WIDE * j : WIDE * j + TILE, :] = jnp.where(live & (lane < 64), block, 0.0).astype(BF)
            out[WIDE * j + TILE : WIDE * j + WIDE, :] = jnp.where(live & (lane >= 64), block, 0.0).astype(BF)

    got(kraw.at[pl.ds(0, 896)], PK)
    stack_heads(kraw, kst)
    got(qraw.at[pl.ds(0, 896)], PQ)
    for i in range(4):
        block = qraw[TILE * i : TILE * i + TILE, :].astype(F32) * 0.0625
        qs[TILE * i : TILE * i + TILE, :] = jnp.where(tile_row < length - TILE * i, block, 0.0).astype(BF)
    got(vraw.at[pl.ds(0, 896)], PV)
    stack_heads(vraw, vst)

    causal = (lax.broadcasted_iota(jnp.int32, (TILE, WIDE), 1) & (TILE - 1)) <= lax.broadcasted_iota(
        jnp.int32, (TILE, WIDE), 0
    )

    def forward(i):
        rows = slice(TILE * i, TILE * i + TILE)
        count = min(i, 3) + 1
        for j in range(count):
            cols = slice(WIDE * j, WIDE * j + WIDE)
            half = dot_nt(qs[rows, :], kst[cols, :])
            twice = 1.0 + jnp.tanh(half)
            weight = half * twice
            slope = 0.5 * twice * (1.0 - weight) + weight
            if i == j:
                weight = jnp.where(causal, weight, 0.0)
                slope = jnp.where(causal, slope, 0.0)
            wst[rows, cols] = weight.astype(BF)
            gst[rows, cols] = slope.astype(BF)
        o_h[rows, :] = dot(wst[rows, : WIDE * count], vst[: WIDE * count, :]).astype(BF)

    for i in range(4):
        forward(i)
    seq_send(PAH, lambda p: o_h.at[rows_at(p, ROWS)], att_r.at[s, pl.ds(0, ROWS)])
    att_r[s, pl.ds(0, ROWS), :] = o_h[rows_at(s, ROWS), :]

    got(qraw.at[pl.ds(HIST, 448)], PTQ)
    for i in range(4, 6):
        rows = slice(TILE * i, TILE * i + TILE)
        qs[rows, :] = (qraw[rows, :].astype(F32) * 0.0625).astype(BF)
        forward(i)
    seq_send(
        PAT,
        lambda p: o_h.at[pl.ds(pl.multiple_of(HIST + p * SLOTS, SLOTS), SLOTS)],
        att_r.at[s, pl.ds(ROWS, SLOTS)],
    )
    att_r[s, pl.ds(ROWS, SLOTS), :] = o_h[target_rows, :]

    def norm(first, gate_ref, gate_first, du_ref):
        rows = pl.ds(pl.multiple_of(first, 32), 32)
        gate_rows = pl.ds(pl.multiple_of(gate_first, 32), 32)
        att = jnp.concatenate([att_r[k, rows, :] for k in range(SEQ)], axis=1).astype(F32)
        centred = att - jnp.mean(att, axis=1, keepdims=True)
        inverse = lax.rsqrt(jnp.mean(centred * centred, axis=1, keepdims=True) + 1e-05)
        normed = centred * inverse
        gate = gate_ref[gate_rows, :].astype(F32)
        gated[rows, :] = (normed * gain[...] * gate).astype(BF)
        scaled = dz[rows, :] * gain[...]
        du_ref[gate_rows, :] = (scaled * normed).astype(BF)
        d_norm = scaled * gate
        d_att = inverse * (
            d_norm
            - jnp.mean(d_norm, axis=1, keepdims=True)
            - normed * jnp.mean(d_norm * normed, axis=1, keepdims=True)
        )
        d_att = d_att.astype(BF)
        for k in range(SEQ):
            datt[k, rows, :] = d_att[:, 128 * k : 128 * k + 128]

    def norm_hist(r, carry):
        norm(r * 32, u_v, r * 32, du_h)
        return carry

    def norm_tgt(r, carry):
        norm(ROWS + r * 32, tgate, r * 32, dgt)
        return carry

    got(att_r.at[pl.ds(0, 7), pl.ds(0, ROWS)], PAH)
    lax.fori_loop(0, 4, norm_hist, 0)
    seq_send(PDH, lambda p: datt.at[p, pl.ds(0, ROWS)], da_raw.at[rows_at(s, ROWS)])
    da_raw[rows_at(s, ROWS), :] = datt[s, pl.ds(0, ROWS), :]
    local(du_h, dqkvu_out.at[:, pl.ds(0, D)], LDU)

    got(att_r.at[pl.ds(0, 7), pl.ds(ROWS, SLOTS)], PAT)
    lax.fori_loop(0, 2, norm_tgt, 0)
    seq_send(PDT, lambda p: datt.at[p, pl.ds(ROWS, SLOTS)], da_raw.at[target_rows])
    da_raw[target_rows, :] = datt[s, pl.ds(ROWS, SLOTS), :]

    gate_stack = jnp.concatenate([dgt[:, 128 * k : 128 * k + 128] for k in range(SEQ)], axis=0)
    zg[...] = dot(perm_back, gate_stack).astype(BF)
    dp_send(PGT, zg, rg)
    rg[rows_at(g, 16), :] = zg[rows_at(g, 16), :]

    other = 1 - core
    p_send[...] = dot_tn(gated[...], cot[:, rows_at(other, 512)]).astype(BF)
    send(p_send, c_recv, PC, {"seq": s + 1 - 2 * core})
    p_own[...] = dot_tn(gated[...], cot[:, rows_at(core, 512)])
    outs[...] = dot(gated[...], w_v[...]).astype(BF)
    local(outs.at[pl.ds(0, ROWS)], ho_out, LHO)
    local(outs.at[pl.ds(ROWS, SLOTS)], to_out, LTO)

    def backward(i):
        rows = slice(TILE * i, TILE * i + TILE)
        count = min(i, 3) + 1
        for j in range(count):
            cols = slice(WIDE * j, WIDE * j + WIDE)
            d_weight = dot_nt(da[rows, :], vst[cols, :])
            dsc[rows, cols] = (d_weight * gst[rows, cols].astype(F32)).astype(BF)
        return (dot(dsc[rows, : WIDE * count], kst[: WIDE * count, :]) * 0.125).astype(BF)

    got(da_raw.at[pl.ds(HIST, 448)], PDT)
    da[HIST:ALL, :] = da_raw[HIST:ALL, :]
    for i in range(4, 6):
        dqt[TILE * (i - 4) : TILE * (i - 3), :] = backward(i)
    seq_send(PQS, lambda p: dqt.at[rows_at(p, SLOTS)], yq.at[rows_at(s, SLOTS)])
    yq[rows_at(s, SLOTS), :] = dqt[rows_at(s, SLOTS), :]

    got(c_recv, PC)
    for d in range(1, NY + 1):
        yp = lax.rem(y + d, NY)
        rows = rows_at(yp, 256)
        total = p_own[rows, :] + c_recv[rows, :].astype(F32)
        if d < NY:
            y_send[yp] = total.astype(BF)
            send(y_send.at[yp], y_recv.at[y], PY, {"dp": yp * NZ + z})
        else:
            y_own[...] = total

    got(da_raw.at[pl.ds(0, 896)], PDH)
    for i in range(4):
        rows = slice(TILE * i, TILE * i + TILE)
        da[rows, :] = jnp.where(tile_row < length - TILE * i, da_raw[rows, :].astype(F32), 0.0).astype(BF)
    for i in range(4):
        gq[TILE * i : TILE * i + TILE, :] = backward(i)

    def grads_send(phase, buf, base):
        place = dqkvu_out.at[:, pl.ds(pl.multiple_of(base + s * 128, 128), 128)]
        seq_send(phase, lambda p: buf.at[rows_at(p, ROWS)], place)
        local(buf.at[rows_at(s, ROWS)], place, LGR)

    grads_send(PGQ, gq, 2 * D)

    def key_sum(left, right, j):
        both = dot_tn(left[TILE * j : ALL, WIDE * j : WIDE * j + WIDE], right[TILE * j : ALL, :])
        return jnp.where(lane < 64, both[:TILE, :], both[TILE:, :])

    for j in range(4):
        gk[TILE * j : TILE * j + TILE, :] = (key_sum(dsc, qs, j) * 2.0).astype(BF)
    grads_send(PGK, gk, 3 * D)
    for j in range(4):
        gv[TILE * j : TILE * j + TILE, :] = key_sum(wst, da, j).astype(BF)
    grads_send(PGV, gv, D)

    got(yq.at[pl.ds(0, 448)], PQS)
    zq[...] = dot(perm_back, yq[...]).astype(BF)
    dp_send(PQD, zq, rq)
    rq[rows_at(g, 16), :] = zq[rows_at(g, 16), :]

    got(y_recv.at[pl.ds(0, NY - 1)], PY)
    total = y_own[...]
    for d in range(1, NY):
        total = total + y_recv[lax.rem(y + d, NY)].astype(F32)
    y_own[...] = total
    for d in range(1, NZ):
        zp = lax.rem(z + d, NZ)
        z_send[zp] = y_own[rows_at(zp, 32), :].astype(BF)
        send(z_send.at[zp], z_recv.at[z], PZ, {"dp": y * NZ + zp})
    z_own[...] = y_own[rows_at(z, 32), :]

    got(rg.at[pl.ds(0, 496)], PGT)
    got(rq.at[pl.ds(0, 496)], PQD)
    returned = jnp.concatenate([rq[...], rg[...]], axis=1)
    d_items = dot(sel_t[...], returned).astype(BF)
    for k in range(SEQ):
        di[:, 128 * k : 128 * k + 128] = d_items[64 * k : 64 * k + 64, :128]
        di[:, D + 128 * k : D + 128 * k + 128] = d_items[64 * k : 64 * k + 64, 128:]
    local(di, di_out, LDI)

    got(z_recv.at[pl.ds(0, NZ - 1)], PZ)
    total = z_own[...]
    for d in range(1, NZ):
        total = total + z_recv[lax.rem(z + d, NZ)].astype(F32)
    x_send[...] = total
    seq_send(PX, lambda p: x_send.at[rows_at(lax.div(p, 2), 8)], x_recv.at[s])
    x_recv[s] = x_send[rows_at(lax.div(s, 2), 8), :]
    got(x_recv.at[pl.ds(0, SEQ - 1)], PX)
    halves = [x_recv[c] + x_recv[2 + c] + x_recv[4 + c] + x_recv[6 + c] for c in range(2)]
    full = jnp.concatenate(halves, axis=1) * (32768.0 ** -0.5)
    dw[...] = jnp.where(core == 0, full[:4, :], full[4:, :])
    local(dw, dw_out, LDW)

    for phase, buf in ((PGQ, gq), (PGK, gk), (PGV, gv)):
        got(buf.at[pl.ds(0, 896)], phase)
        sent(buf.at[pl.ds(0, 896)], phase)
        local_wait(buf.at[pl.ds(0, ROWS)], LGR)
    for phase, buf in ((PK, kraw), (PQ, qraw), (PV, vraw), (PAH, o_h), (PDH, da_raw)):
        sent(buf.at[pl.ds(0, 896)], phase)
    for phase, buf in ((PTQ, tq), (PAT, o_h), (PDT, da_raw), (PQS, dqt)):
        sent(buf.at[pl.ds(0, 448)], phase)
    for phase, buf in ((PT, tsend), (PGT, zg), (PQD, zq)):
        sent(buf.at[pl.ds(0, 496)], phase)
    sent(p_send, PC)
    sent(y_send.at[pl.ds(0, NY - 1)], PY)
    sent(z_send.at[pl.ds(0, NZ - 1)], PZ)
    sent(x_recv.at[pl.ds(0, SEQ - 1)], PX)
    local_wait(du_h, LDU)
    local_wait(outs.at[pl.ds(0, ROWS)], LHO)
    local_wait(outs.at[pl.ds(ROWS, SLOTS)], LTO)
    local_wait(di, LDI)
    local_wait(dw, LDW)


def scratch():
    def vm(*shape, dtype=BF):
        return pltpu.VMEM(shape, dtype)

    return [
        vm(HIST, 128), vm(HIST, 128), vm(ALL, 128), vm(ALL, 128),
        vm(2 * HIST, 128), vm(2 * HIST, 128),
        vm(ALL, 2 * HIST), vm(ALL, 2 * HIST), vm(ALL, 2 * HIST),
        vm(ROWS, D), vm(D, D), vm(ROWS + SLOTS, D), vm(ROWS + SLOTS, D, dtype=F32),
        vm(512, 512), vm(512, 256), vm(512, 256), vm(512, 128), vm(SLOTS, D),
        vm(ALL, 128), vm(SEQ, ROWS + SLOTS, 128), vm(SEQ, ROWS + SLOTS, 128),
        vm(ALL, 128), vm(ALL, 128),
        vm(ROWS + SLOTS, D), vm(ROWS + SLOTS, D), vm(ROWS, D), vm(SLOTS, D),
        vm(512, 128), vm(512, 128), vm(512, 128), vm(512, 128), vm(512, 128), vm(512, 128),
        vm(HIST, 128), vm(HIST, 128), vm(HIST, 128), vm(SLOTS, 2 * D),
        vm(D, 512), vm(D, 512, dtype=F32), vm(D, 512),
        vm(NY, 256, 512), vm(256, 512, dtype=F32), vm(NY, 256, 512),
        vm(NZ, 32, 512), vm(32, 512, dtype=F32), vm(NZ, 32, 512),
        vm(32, 512, dtype=F32), vm(SEQ, 8, 512, dtype=F32), vm(4, D, dtype=F32),
        pltpu.SemaphoreType.DMA((NPH,)),
        pltpu.SemaphoreType.DMA((NPH,)),
        pltpu.SemaphoreType.DMA((NLOC,)),
    ]


def shards(qkvu, lengths, items, send_list, send_count, w_out, gain, g_hist, g_tgt):
    lists, counts = send_list[0, 0], send_count[0, 0]
    slot = lax.broadcasted_iota(jnp.int32, (DP, SEQ, 2), 2)
    block = lax.broadcasted_iota(jnp.int32, (DP, SEQ, 2), 1)
    code = jnp.where(slot < counts[:, None, None], block * SLOTS + lists[:, None, :], -1).reshape(1, 512)
    anywhere = pl.BlockSpec(memory_space=pl.ANY)
    vmem = pl.BlockSpec(memory_space=pltpu.VMEM)
    hist_out, tgt_out, d_qkvu, d_items, d_w2 = pl.pallas_call(
        kernel,
        out_shape=(
            jax.ShapeDtypeStruct((ROWS, D), BF),
            jax.ShapeDtypeStruct((SLOTS, D), BF),
            jax.ShapeDtypeStruct((ROWS, 4 * D), BF),
            jax.ShapeDtypeStruct((SLOTS, 2 * D), BF),
            jax.ShapeDtypeStruct((4, D), F32),
        ),
        in_specs=[vmem, pl.BlockSpec(memory_space=pltpu.SMEM), anywhere, vmem, anywhere, vmem, anywhere, anywhere],
        out_specs=(anywhere,) * 5,
        scratch_shapes=scratch(),
        compiler_params=pltpu.CompilerParams(
            collective_id=0, has_side_effects=True, vmem_limit_bytes=60 * 1024 * 1024
        ),
    )(code, lengths, qkvu[0], items[0, 0], w_out, gain.reshape(1, D), g_hist[0], g_tgt.reshape(SLOTS, D))
    return (
        hist_out[None],
        tgt_out.reshape(1, 1, DP, 2, D),
        d_qkvu[None],
        d_items[None, None],
        d_w2,
    )


def solution(mesh):
    in_specs = (
        P("dp", "seq", None),
        P("dp"),
        P("dp", "seq", None, None),
        P("dp", "seq", None, None),
        P("dp", "seq", None),
        P(),
        P(),
        P("dp", "seq", None),
        P("dp", "seq", None, None, None),
    )
    out_specs = (
        P("dp", "seq", None),
        P("dp", "seq", None, None, None),
        P("dp", "seq", None),
        P("dp", "seq", None, None),
        P(("dp", "seq"), None),
    )
    return jax.shard_map(shards, mesh=mesh, in_specs=in_specs, out_specs=out_specs, check_vma=False)
```

time: 452 us -> 81.4 us (0.18)
  waiting for transfers between devices: 245 us -> 0 us
  Pallas kernels: 0 us -> 69.1 us
  local copies, waits for them, and re-layouts: 72.3 us -> 10 us
  other arithmetic: 50.3 us -> 0.76 us
  matrix products: 46.9 us -> 0 us
  starting transfers between devices: 21.8 us -> 0 us
  between operations: 14.2 us -> 1.32 us
    unnamed x5 -> x0, waiting for transfers between devices: 146 us -> none
    pallas_call x0 -> x1, Pallas kernels: none -> 69.1 us  [shards(): pl.pallas_call(kernel, out_shape=(jax.ShapeDtypeStruct((ROWS, D), BF), ja...]
    reduce_scatter x1 -> x0, waiting for transfers between devices: 55.9 us -> none  [shards(): lax.psum_scatter(key_terms, 'seq', scatter_dimension=0, tiled=True)]
    dot_general x28 -> x0, matrix products: 46.9 us -> none  [the longest x4 14.1 us: tile_sum(): jnp.einsum('hqk,khe->qhe', weight, value_tile, preferred_element_type=jnp...]
    all_gather x2 -> x0, waiting for transfers between devices: 30.8 us -> none  [the longest x1 26 us: shards(): lax.all_gather(history[:, width:2 * width], 'seq', axis=0, tiled=True)]
    all_to_all x2 -> x0, starting transfers between devices: 21.6 us -> none  [the longest x1 12 us: shards(): lax.all_to_all(picked, 'dp', split_axis=0, concat_axis=0, tiled=True)]
    while x52 -> x0, local copies, waits for them, and re-layouts: 21.6 us -> none
    another operation x7 -> x0, local copies, waits for them, and re-layouts: 21 us -> none  [the longest x2 10.9 us: shards(): jnp.stack([(gv_hist + gv_tgt).reshape(span, width), (gk_hist + gk_tgt).re...]
  transfers between devices with their start and end apart: 6 -> 0, of which waited for: 6 -> 0; matrix products, arithmetic and copies ran while one was open for 21% -> 0% of each run, Pallas kernels for 0% -> 0%
where the time goes in v1:
time: 81.4 us; the launch traced here: 81.2 us
  Pallas kernels  69.1 us (85%)
  local copies, waits for them, and re-layouts  10 us (12%)
  between operations  1.32 us (2%)
    pallas_call x1, Pallas kernels, shards(): pl.pallas_call(kernel, out_shape=(jax.ShapeDtypeStruct((ROWS, D), BF), ja...  69.1 us
    unnamed x8, local copies, waits for them, and re-layouts  5.27 us
    reshape x1, local copies, waits for them, and re-layouts, shards(): tgt_out.reshape(1, 1, DP, 2, D)  1.65 us

profile of v1, /device:TPU:1, one launch (start us, length us, event | category | flops | bytes accessed | tf_op | source)
XLA Modules:
  0.0 81.2 jit_solution(8939769691197601404)
XLA Ops:
  1.3 0.8 copy.15
  2.1 0.8 add_select_fusion
  2.8 0.7 select_n.15.code
  3.5 1.6 %reshape.72.gt_hbm = bf16[64,1024]{1,0:T(8,128)(2,1)} reshape(bf16[1,1,32,2,1024]{4,3,2,1,0:T(2,128)(2,1)} %param.17) | data formatting | bytes 262144 | tf_op jit(solution)/shard_map/reshape | solution.py:420
  5.1 69.1 %shard_map.128 = (bf16[128,1024]{1,0:T(8,128)(2,1)}, bf16[64,1024]{1,0:T(8,128)(2,1)}, bf16[128,4096]{1,0:T(8,128)(2,1)}, bf16[64,2048]{1,0:T(8,128)(2,1)}, f32[4,1024]{1,0:T(4,128)}) custom-call(s32[1,512]{1,0:T(1,128)} %select_n.15.code, s32[1]{0:T(128)S(6)} %copy.20.length_ref, bf16[128,4096]{1,0:T(8,128)(2,1)} %bitcast.9, bf16[64,2048]{1,0:T(8,128)(2,1)} %bitcast.11, ...), custom_call_target="tpu_custom_call" | custom-call | tf_op jit(solution)/shard_map/pallas_call | solution.py:405
  74.2 0.0 copy-start
  74.2 0.0 copy-start.1
  74.2 1.7 %reshape.73 = bf16[1,1,32,2,1024]{4,3,2,1,0:T(2,128)(2,1)} reshape(bf16[64,1024]{1,0:T(8,128)(2,1)} %get-tuple-element.11) | data formatting | bytes 262144 | tf_op jit(solution)/shard_map/reshape | solution.py:423
  75.9 1.7 %copy.21 = bf16[1,128,1024]{2,1,0:T(8,128)(2,1)} copy(bf16[1,128,1024]{2,1,0:T(8,128)(2,1)} %bitcast.14) | data formatting | bytes 524288
  77.6 2.3 %copy.22 = bf16[1,128,4096]{2,1,0:T(8,128)(2,1)} copy(bf16[1,128,4096]{2,1,0:T(8,128)(2,1)} %bitcast.10) | data formatting | bytes 2097152
  79.8 0.0 copy-done
  79.8 0.7 copy.23
  80.5 0.0 copy-done.1
  80.5 0.6 copy.24
  (1 shorter events, 0.0 us)
Async XLA Ops:
  74.2 5.6 %copy-start = (bf16[64,2048]{1,0:T(8,128)(2,1)S(1)}, bf16[64,2048]{1,0:T(8,128)(2,1)}, u32[]{:S(2)}) copy-start(bf16[64,2048]{1,0:T(8,128)(2,1)} %get-tuple-element.13) | copy-start | bytes 786436
  74.2 6.3 %copy-start.1 = (f32[4,1024]{1,0:T(4,128)S(1)}, f32[4,1024]{1,0:T(4,128)}, u32[]{:S(2)}) copy-start(f32[4,1024]{1,0:T(4,128)} %get-tuple-element.24) | copy-start | bytes 49156

commit v2 on v1

--- a/solution.py
+++ b/solution.py
@@ -21,8 +21,8 @@
 TILE = 256
 WIDE = 2 * TILE
 
-(PK, PQ, PV, PT, PTQ, PAH, PAT, PDH, PDT, PGT, PQS, PQD, PGQ, PGK, PGV, PC, PY, PZ, PX, NPH) = range(20)
-(LIN, LW, LCOT, LU, LHO, LTO, LDU, LGR, LDI, LDW, NLOC) = range(11)
+(PK, PQ, PV, PT, PTQ, PAH, PAT, PDH, PDT, PGT, PQS, PQD, PGQ, PGK, PGV, PCO, PGA, PGB, PZ, PX, NPH) = range(21)
+(LLI, LCO, LIT, LGA, LIN, LW, LCOT, LGT, LU, LHO, LTO, LDU, LGR, LDI, LDW, NLOC) = range(16)
 
 
 def dot(a, b):
@@ -42,18 +42,20 @@
 
 
 def kernel(
-    code, length_ref, qkvu, items, w_hbm, gain, gh_hbm, gt_hbm,
+    lists_hbm, counts_hbm, length_ref, qkvu, items_hbm, w_hbm, gain_hbm, gh_hbm, gt_hbm,
     ho_out, to_out, dqkvu_out, di_out, dw_out,
     kraw, vraw, qraw, qs, kst, vst, wst, gst, dsc,
-    u_v, w_v, cot, dz, sel_t, tsend, trecv, tq, tgate,
+    lists, counts, items, gain, u_v, w_v, gt_v, to_v, rows32, cot, dz, sel_t, tsend, trecv, tq, tgate,
     o_h, att_r, datt, da_raw, da, gated, outs, du_h, dgt, zg, rg, dqt, yq, zq, rq,
-    gq, gk, gv, di, p_send, p_own, c_recv, y_send, y_own, y_recv, z_send, z_own, z_recv, x_send, x_recv, dw,
+    gq, gk, gv, di, cot_all, gated_all, y_own, z_send, z_own, z_recv, x_send, x_recv, dw,
     ssem, rsem, lsem,
 ):
     g = lax.axis_index("dp")
     s = lax.axis_index("seq")
     y, z = lax.div(g, NZ), lax.rem(g, NZ)
     core = lax.rem(s, 2)
+    other = s + 1 - 2 * core
+    mine = 2 * y + core
     length = length_ref[0]
 
     def rows_at(index, size):
@@ -68,6 +70,10 @@
     for d in range(1, SEQ):
         pl.semaphore_signal(barrier, inc=1, device_id={"seq": lax.rem(s + d, SEQ)}, device_id_type=MESH)
     lax.fori_loop(1, DP, greet_dp, 0)
+    for d in range(1, NY):
+        pl.semaphore_signal(
+            barrier, inc=1, device_id={"dp": lax.rem(y + d, NY) * NZ + z, "seq": other}, device_id_type=MESH
+        )
 
     def local(src, dst, sem):
         copy = pltpu.make_async_copy(src, dst, lsem.at[sem])
@@ -93,14 +99,32 @@
     def sent(ref, phase):
         pltpu.make_async_copy(ref, ref, ssem.at[phase]).wait()
 
+    local(lists_hbm, lists, LLI)
+    local(counts_hbm, counts, LCO)
+    local(items_hbm, items, LIT)
+    local(gain_hbm, gain, LGA)
     for base, buf in ((3 * D, kraw), (2 * D, qraw), (D, vraw)):
         local(qkvu.at[:, pl.ds(pl.multiple_of(base + s * 128, 128), 128)], buf.at[rows_at(s, ROWS)], LIN)
     local(w_hbm, w_v, LW)
     local(gh_hbm, cot.at[pl.ds(0, ROWS)], LCOT)
-    local(gt_hbm, cot.at[pl.ds(ROWS, SLOTS)], LCOT)
+    local(gt_hbm, gt_v, LGT)
     local(qkvu.at[:, pl.ds(0, D)], u_v, LU)
 
-    sel_t[...] = one_hot(lax.broadcasted_iota(jnp.int32, (512, 512), 0) == code[...])
+    local_wait(lists, LLI)
+    local_wait(counts, LCO)
+    lane512 = lax.broadcasted_iota(jnp.int32, (DP, 512), 1)
+    spread = one_hot((lane512 >> 4) == lax.broadcasted_iota(jnp.int32, (DP, 512), 0))
+
+    def spread_row(row):
+        return dot(jnp.broadcast_to(row.astype(F32), (16, DP)).astype(BF), spread)[:1, :]
+
+    slot = lax.broadcasted_iota(jnp.int32, (1, 512), 1)
+    second = (slot & 1) == 1
+    picked = jnp.where(second, spread_row(lists[1:2, :]), spread_row(lists[0:1, :]))
+    live = spread_row(counts[...]) > jnp.where(second, 1.5, 0.5)
+    code = jnp.where(live, picked + (((slot >> 1) & 7) * SLOTS).astype(F32), -1.0)
+    sel_t[...] = one_hot(lax.broadcasted_iota(jnp.int32, (512, 512), 0).astype(F32) == code)
+    local_wait(items, LIT)
     stacked = jnp.concatenate(
         [
             jnp.concatenate([items[:, 128 * k : 128 * k + 128], items[:, D + 128 * k : D + 128 * k + 128]], axis=1)
@@ -110,7 +134,7 @@
     )
     tsend[...] = dot_tn(sel_t[...], stacked).astype(BF)
 
-    pl.semaphore_wait(barrier, SEQ - 1 + DP - 1)
+    pl.semaphore_wait(barrier, SEQ - 1 + DP - 1 + NY - 1)
 
     def dp_send(phase, src, dst):
         def one(d, carry):
@@ -120,18 +144,23 @@
 
         lax.fori_loop(1, DP, one, 0)
 
-    for phase, base, buf in ((PK, 3 * D, kraw), (PQ, 2 * D, qraw), (PV, D, vraw)):
+    def columns_send(phase, base, buf):
         seq_send(
-            phase,
-            lambda p, base=base: qkvu.at[:, pl.ds(pl.multiple_of(base + p * 128, 128), 128)],
-            buf.at[rows_at(s, ROWS)],
+            phase, lambda p: qkvu.at[:, pl.ds(pl.multiple_of(base + p * 128, 128), 128)], buf.at[rows_at(s, ROWS)]
         )
+
+    columns_send(PK, 3 * D, kraw)
     dp_send(PT, tsend, trecv)
+    columns_send(PQ, 2 * D, qraw)
+    columns_send(PV, D, vraw)
     trecv[rows_at(g, 16), :] = tsend[rows_at(g, 16), :]
 
     local_wait(w_v, LW)
-    local_wait(cot, LCOT)
-    local_wait(u_v, LU)
+    local_wait(cot.at[pl.ds(0, ROWS)], LCOT)
+    local_wait(gt_v, LGT)
+    for h in range(DP):
+        rows32[2 * h : 2 * h + 2, :] = gt_v[h].astype(F32)
+    cot[ROWS:, :] = rows32[...].astype(BF)
     dz[...] = dot_nt(cot[...], w_v[...])
 
     row512 = lax.broadcasted_iota(jnp.int32, (512, 512), 0)
@@ -148,6 +177,17 @@
     seq_send(PTQ, lambda p: tq.at[rows_at(p, SLOTS)], qraw.at[target_rows])
     qraw[target_rows, :] = tq[rows_at(s, SLOTS), :]
 
+    def group_send(phase, src, dst):
+        for d in range(1, 2 * NY):
+            r = lax.rem(mine + d, 2 * NY)
+            ry, rc = lax.div(r, 2), lax.rem(r, 2)
+            send(src(ry, rc), dst, phase, {"dp": ry * NZ + z, "seq": s - core + rc})
+
+    group_send(PCO, lambda ry, rc: cot.at[:, rows_at(rc, 512)], cot_all.at[mine])
+    cot_all[mine] = cot[:, rows_at(core, 512)]
+    local_wait(u_v, LU)
+    local_wait(gain, LGA)
+
     for buf in (kraw, qraw, vraw):
         local_wait(buf.at[pl.ds(0, ROWS)], LIN)
     lane = lax.broadcasted_iota(jnp.int32, (TILE, 128), 1)
@@ -166,14 +206,12 @@
     for i in range(4):
         block = qraw[TILE * i : TILE * i + TILE, :].astype(F32) * 0.0625
         qs[TILE * i : TILE * i + TILE, :] = jnp.where(tile_row < length - TILE * i, block, 0.0).astype(BF)
-    got(vraw.at[pl.ds(0, 896)], PV)
-    stack_heads(vraw, vst)
 
     causal = (lax.broadcasted_iota(jnp.int32, (TILE, WIDE), 1) & (TILE - 1)) <= lax.broadcasted_iota(
         jnp.int32, (TILE, WIDE), 0
     )
 
-    def forward(i):
+    def scores(i):
         rows = slice(TILE * i, TILE * i + TILE)
         count = min(i, 3) + 1
         for j in range(count):
@@ -187,10 +225,18 @@
                 slope = jnp.where(causal, slope, 0.0)
             wst[rows, cols] = weight.astype(BF)
             gst[rows, cols] = slope.astype(BF)
+
+    def attend(i):
+        rows = slice(TILE * i, TILE * i + TILE)
+        count = min(i, 3) + 1
         o_h[rows, :] = dot(wst[rows, : WIDE * count], vst[: WIDE * count, :]).astype(BF)
 
     for i in range(4):
-        forward(i)
+        scores(i)
+    got(vraw.at[pl.ds(0, 896)], PV)
+    stack_heads(vraw, vst)
+    for i in range(4):
+        attend(i)
     seq_send(PAH, lambda p: o_h.at[rows_at(p, ROWS)], att_r.at[s, pl.ds(0, ROWS)])
     att_r[s, pl.ds(0, ROWS), :] = o_h[rows_at(s, ROWS), :]
 
@@ -198,7 +244,8 @@
     for i in range(4, 6):
         rows = slice(TILE * i, TILE * i + TILE)
         qs[rows, :] = (qraw[rows, :].astype(F32) * 0.0625).astype(BF)
-        forward(i)
+        scores(i)
+        attend(i)
     seq_send(
         PAT,
         lambda p: o_h.at[pl.ds(pl.multiple_of(HIST + p * SLOTS, SLOTS), SLOTS)],
@@ -240,6 +287,9 @@
     seq_send(PDH, lambda p: datt.at[p, pl.ds(0, ROWS)], da_raw.at[rows_at(s, ROWS)])
     da_raw[rows_at(s, ROWS), :] = datt[s, pl.ds(0, ROWS), :]
     local(du_h, dqkvu_out.at[:, pl.ds(0, D)], LDU)
+    hist_rows = pl.ds(0, ROWS)
+    slot_rows = pl.ds(ROWS, SLOTS)
+    group_send(PGA, lambda ry, rc: gated.at[hist_rows, rows_at(ry, 256)], gated_all.at[mine, hist_rows])
 
     got(att_r.at[pl.ds(0, 7), pl.ds(ROWS, SLOTS)], PAT)
     lax.fori_loop(0, 2, norm_tgt, 0)
@@ -251,13 +301,14 @@
     dp_send(PGT, zg, rg)
     rg[rows_at(g, 16), :] = zg[rows_at(g, 16), :]
 
-    other = 1 - core
-    p_send[...] = dot_tn(gated[...], cot[:, rows_at(other, 512)]).astype(BF)
-    send(p_send, c_recv, PC, {"seq": s + 1 - 2 * core})
-    p_own[...] = dot_tn(gated[...], cot[:, rows_at(core, 512)])
-    outs[...] = dot(gated[...], w_v[...]).astype(BF)
-    local(outs.at[pl.ds(0, ROWS)], ho_out, LHO)
-    local(outs.at[pl.ds(ROWS, SLOTS)], to_out, LTO)
+    group_send(PGB, lambda ry, rc: gated.at[slot_rows, rows_at(ry, 256)], gated_all.at[mine, slot_rows])
+    gated_all[mine] = gated[:, rows_at(y, 256)]
+    outs[...] = dot(gated[:ROWS, :], w_v[...]).astype(BF)
+    local(outs, ho_out, LHO)
+    rows32[...] = dot(gated[ROWS:, :], w_v[...])
+    for h in range(DP):
+        to_v[h] = rows32[2 * h : 2 * h + 2, :].astype(BF)
+    local(to_v, to_out, LTO)
 
     def backward(i):
         rows = slice(TILE * i, TILE * i + TILE)
@@ -275,17 +326,6 @@
     seq_send(PQS, lambda p: dqt.at[rows_at(p, SLOTS)], yq.at[rows_at(s, SLOTS)])
     yq[rows_at(s, SLOTS), :] = dqt[rows_at(s, SLOTS), :]
 
-    got(c_recv, PC)
-    for d in range(1, NY + 1):
-        yp = lax.rem(y + d, NY)
-        rows = rows_at(yp, 256)
-        total = p_own[rows, :] + c_recv[rows, :].astype(F32)
-        if d < NY:
-            y_send[yp] = total.astype(BF)
-            send(y_send.at[yp], y_recv.at[y], PY, {"dp": yp * NZ + z})
-        else:
-            y_own[...] = total
-
     got(da_raw.at[pl.ds(0, 896)], PDH)
     for i in range(4):
         rows = slice(TILE * i, TILE * i + TILE)
@@ -316,11 +356,10 @@
     dp_send(PQD, zq, rq)
     rq[rows_at(g, 16), :] = zq[rows_at(g, 16), :]
 
-    got(y_recv.at[pl.ds(0, NY - 1)], PY)
-    total = y_own[...]
-    for d in range(1, NY):
-        total = total + y_recv[lax.rem(y + d, NY)].astype(F32)
-    y_own[...] = total
+    got(cot_all.at[pl.ds(0, 7)], PCO)
+    got(gated_all.at[pl.ds(0, 7), hist_rows], PGA)
+    got(gated_all.at[pl.ds(0, 7), slot_rows], PGB)
+    y_own[...] = dot_tn(gated_all[...].reshape(8 * 192, 256), cot_all[...].reshape(8 * 192, 512))
     for d in range(1, NZ):
         zp = lax.rem(z + d, NZ)
         z_send[zp] = y_own[rows_at(zp, 32), :].astype(BF)
@@ -359,15 +398,26 @@
         sent(buf.at[pl.ds(0, 448)], phase)
     for phase, buf in ((PT, tsend), (PGT, zg), (PQD, zq)):
         sent(buf.at[pl.ds(0, 496)], phase)
-    sent(p_send, PC)
-    sent(y_send.at[pl.ds(0, NY - 1)], PY)
+    sent(cot_all.at[pl.ds(0, 7)], PCO)
+    sent(gated_all.at[pl.ds(0, 7), hist_rows], PGA)
+    sent(gated_all.at[pl.ds(0, 7), slot_rows], PGB)
     sent(z_send.at[pl.ds(0, NZ - 1)], PZ)
     sent(x_recv.at[pl.ds(0, SEQ - 1)], PX)
     local_wait(du_h, LDU)
-    local_wait(outs.at[pl.ds(0, ROWS)], LHO)
-    local_wait(outs.at[pl.ds(ROWS, SLOTS)], LTO)
+    local_wait(outs, LHO)
+    local_wait(to_v, LTO)
     local_wait(di, LDI)
     local_wait(dw, LDW)
+
+
+def deliver(ho, to, dqkvu, di, dw, ho_out, to_out, dqkvu_out, di_out, dw_out, sem):
+    pairs = [(dqkvu.at[pl.ds(32 * r, 32)], dqkvu_out.at[pl.ds(32 * r, 32)]) for r in range(4)]
+    pairs += [(ho, ho_out), (to, to_out), (di, di_out), (dw, dw_out)]
+    copies = [pltpu.make_async_copy(a, b, sem.at[n]) for n, (a, b) in enumerate(pairs)]
+    for copy in copies:
+        copy.start()
+    for copy in copies:
+        copy.wait()
 
 
 def scratch():
@@ -378,15 +428,16 @@
         vm(HIST, 128), vm(HIST, 128), vm(ALL, 128), vm(ALL, 128),
         vm(2 * HIST, 128), vm(2 * HIST, 128),
         vm(ALL, 2 * HIST), vm(ALL, 2 * HIST), vm(ALL, 2 * HIST),
-        vm(ROWS, D), vm(D, D), vm(ROWS + SLOTS, D), vm(ROWS + SLOTS, D, dtype=F32),
+        vm(2, DP, dtype=jnp.int32), vm(1, DP, dtype=jnp.int32), vm(SLOTS, 2 * D), vm(1, D, dtype=F32),
+        vm(ROWS, D), vm(D, D), vm(DP, 2, D), vm(DP, 2, D), vm(SLOTS, D, dtype=F32),
+        vm(ROWS + SLOTS, D), vm(ROWS + SLOTS, D, dtype=F32),
         vm(512, 512), vm(512, 256), vm(512, 256), vm(512, 128), vm(SLOTS, D),
         vm(ALL, 128), vm(SEQ, ROWS + SLOTS, 128), vm(SEQ, ROWS + SLOTS, 128),
         vm(ALL, 128), vm(ALL, 128),
-        vm(ROWS + SLOTS, D), vm(ROWS + SLOTS, D), vm(ROWS, D), vm(SLOTS, D),
+        vm(ROWS + SLOTS, D), vm(ROWS, D), vm(ROWS, D), vm(SLOTS, D),
         vm(512, 128), vm(512, 128), vm(512, 128), vm(512, 128), vm(512, 128), vm(512, 128),
         vm(HIST, 128), vm(HIST, 128), vm(HIST, 128), vm(SLOTS, 2 * D),
-        vm(D, 512), vm(D, 512, dtype=F32), vm(D, 512),
-        vm(NY, 256, 512), vm(256, 512, dtype=F32), vm(NY, 256, 512),
+        vm(8, ROWS + SLOTS, 512), vm(8, ROWS + SLOTS, 256), vm(256, 512, dtype=F32),
         vm(NZ, 32, 512), vm(32, 512, dtype=F32), vm(NZ, 32, 512),
         vm(32, 512, dtype=F32), vm(SEQ, 8, 512, dtype=F32), vm(4, D, dtype=F32),
         pltpu.SemaphoreType.DMA((NPH,)),
@@ -396,31 +447,37 @@
 
 
 def shards(qkvu, lengths, items, send_list, send_count, w_out, gain, g_hist, g_tgt):
-    lists, counts = send_list[0, 0], send_count[0, 0]
-    slot = lax.broadcasted_iota(jnp.int32, (DP, SEQ, 2), 2)
-    block = lax.broadcasted_iota(jnp.int32, (DP, SEQ, 2), 1)
-    code = jnp.where(slot < counts[:, None, None], block * SLOTS + lists[:, None, :], -1).reshape(1, 512)
-    anywhere = pl.BlockSpec(memory_space=pl.ANY)
+    hbm = pl.BlockSpec(memory_space=pltpu.HBM)
     vmem = pl.BlockSpec(memory_space=pltpu.VMEM)
-    hist_out, tgt_out, d_qkvu, d_items, d_w2 = pl.pallas_call(
+    results = pl.pallas_call(
         kernel,
         out_shape=(
-            jax.ShapeDtypeStruct((ROWS, D), BF),
-            jax.ShapeDtypeStruct((SLOTS, D), BF),
-            jax.ShapeDtypeStruct((ROWS, 4 * D), BF),
-            jax.ShapeDtypeStruct((SLOTS, 2 * D), BF),
-            jax.ShapeDtypeStruct((4, D), F32),
+            pltpu.VMEM((ROWS, D), BF),
+            pltpu.VMEM((DP, 2, D), BF),
+            pltpu.VMEM((ROWS, 4 * D), BF),
+            pltpu.VMEM((SLOTS, 2 * D), BF),
+            pltpu.VMEM((4, D), F32),
         ),
-        in_specs=[vmem, pl.BlockSpec(memory_space=pltpu.SMEM), anywhere, vmem, anywhere, vmem, anywhere, anywhere],
-        out_specs=(anywhere,) * 5,
+        in_specs=[hbm, hbm, pl.BlockSpec(memory_space=pltpu.SMEM)] + [hbm] * 6,
+        out_specs=(vmem,) * 5,
         scratch_shapes=scratch(),
         compiler_params=pltpu.CompilerParams(
-            collective_id=0, has_side_effects=True, vmem_limit_bytes=60 * 1024 * 1024
+            collective_id=0, has_side_effects=True, vmem_limit_bytes=56 * 1024 * 1024
         ),
-    )(code, lengths, qkvu[0], items[0, 0], w_out, gain.reshape(1, D), g_hist[0], g_tgt.reshape(SLOTS, D))
+    )(
+        send_list[0, 0].T, send_count[0], lengths, qkvu[0], items[0, 0], w_out, gain.reshape(1, D), g_hist[0], g_tgt[0, 0]
+    )
+    hist_out, tgt_out, d_qkvu, d_items, d_w2 = pl.pallas_call(
+        deliver,
+        out_shape=tuple(jax.ShapeDtypeStruct(r.shape, r.dtype) for r in results),
+        in_specs=(vmem,) * 5,
+        out_specs=(hbm,) * 5,
+        scratch_shapes=[pltpu.SemaphoreType.DMA((8,))],
+        compiler_params=pltpu.CompilerParams(vmem_limit_bytes=8 * 1024 * 1024),
+    )(*results)
     return (
         hist_out[None],
-        tgt_out.reshape(1, 1, DP, 2, D),
+        tgt_out[None, None],
         d_qkvu[None],
         d_items[None, None],
         d_w2,

time: 81.4 us -> 67.6 us (0.83)
  local copies, waits for them, and re-layouts: 10 us -> 0 us
  Pallas kernels: 69.1 us -> 66.1 us
    unnamed x8 -> x0, local copies, waits for them, and re-layouts: 5.27 us -> none
    reshape x2 -> x0, local copies, waits for them, and re-layouts: 3.26 us -> none  [the longest x1 1.65 us: shards(): tgt_out.reshape(1, 1, DP, 2, D)]
    pallas_call x1 -> x2, Pallas kernels: 69.1 us -> 66.1 us  [the longest x1 64.8 us: shards(): pl.pallas_call(kernel, out_shape=(pltpu.VMEM((ROWS, D), BF), pltpu.VMEM((...]
where the time goes in v2:
time: 67.6 us; the launch traced here: 67.5 us
  Pallas kernels  66.1 us (98%)
  between operations  1.45 us (2%)
    pallas_call x1, Pallas kernels, shards(): pl.pallas_call(kernel, out_shape=(pltpu.VMEM((ROWS, D), BF), pltpu.VMEM((...  64.8 us

profile of v2, /device:TPU:1, one launch (start us, length us, event | category | flops | bytes accessed | tf_op | source)
XLA Modules:
  0.0 67.5 jit_solution(16190021568331303396)
XLA Ops:
  1.3 64.8 %shard_map.128 = (bf16[128,1024]{1,0:T(8,128)(2,1)S(1)}, bf16[32,2,1024]{2,1,0:T(2,128)(2,1)S(1)}, bf16[128,4096]{1,0:T(8,128)(2,1)S(1)}, bf16[64,2048]{1,0:T(8,128)(2,1)S(1)}, f32[4,1024]{1,0:T(4,128)S(1)}) custom-call(s32[2,32]{1,0:T(2,128)} %bitcast.18, s32[1,32]{1,0:T(1,128)} %bitcast.19, s32[1]{0:T(128)S(6)} %copy.14.length_ref, ...), custom_call_target="tpu_custom_call" | custom-call | tf_op jit(solution)/shard_map/pallas_call | solution.py:452
  66.1 1.3 %shard_map.129 = (bf16[128,1024]{1,0:T(8,128)(2,1)}, bf16[32,2,1024]{2,1,0:T(2,128)(2,1)}, bf16[128,4096]{1,0:T(8,128)(2,1)}, bf16[64,2048]{1,0:T(8,128)(2,1)}, f32[4,1024]{1,0:T(4,128)}) custom-call(bf16[128,1024]{1,0:T(8,128)(2,1)S(1)} %get-tuple-element.15.ho, bf16[32,2,1024]{2,1,0:T(2,128)(2,1)S(1)} %get-tuple-element.16.to, ...), custom_call_target="tpu_custom_call" | custom-call | tf_op jit(solution)/shard_map/pallas_call | solution.py:470

commit v3 on v2

--- a/solution.py
+++ b/solution.py
@@ -21,7 +21,7 @@
 TILE = 256
 WIDE = 2 * TILE
 
-(PK, PQ, PV, PT, PTQ, PAH, PAT, PDH, PDT, PGT, PQS, PQD, PGQ, PGK, PGV, PCO, PGA, PGB, PZ, PX, NPH) = range(21)
+(PK, PQ, PV, PT, PTQ, PAH, PAT, PDH, PDT, PSH, PST, PGT, PQS, PQD, PGQ, PGK, PGV, PCO, PCF, PGA, PGB, PZ, PX, NPH) = range(24)
 (LLI, LCO, LIT, LGA, LIN, LW, LCOT, LGT, LU, LHO, LTO, LDU, LGR, LDI, LDW, NLOC) = range(16)
 
 
@@ -47,12 +47,13 @@
     kraw, vraw, qraw, qs, kst, vst, wst, gst, dsc,
     lists, counts, items, gain, u_v, w_v, gt_v, to_v, rows32, cot, dz, sel_t, tsend, trecv, tq, tgate,
     o_h, att_r, datt, da_raw, da, gated, outs, du_h, dgt, zg, rg, dqt, yq, zq, rq,
-    gq, gk, gv, di, cot_all, gated_all, y_own, z_send, z_own, z_recv, x_send, x_recv, dw,
+    gq, gk, gv, di, st_hs, st_ts, st_h, st_t, gated_p, cot_all, gated_all, y_own, z_send, z_recv, x_send, x_recv, dw,
     ssem, rsem, lsem,
 ):
     g = lax.axis_index("dp")
     s = lax.axis_index("seq")
     y, z = lax.div(g, NZ), lax.rem(g, NZ)
+    x = lax.div(s, 2)
     core = lax.rem(s, 2)
     other = s + 1 - 2 * core
     mine = 2 * y + core
@@ -161,7 +162,32 @@
     for h in range(DP):
         rows32[2 * h : 2 * h + 2, :] = gt_v[h].astype(F32)
     cot[ROWS:, :] = rows32[...].astype(BF)
+    for d in range(1, NY):
+        send(cot, cot_all.at[mine], PCO, {"dp": lax.rem(y + d, NY) * NZ + z})
+    send(cot, cot_all.at[mine], PCF, {"seq": other})
     dz[...] = dot_nt(cot[...], w_v[...])
+
+    def d_norm(first, gate_ref, gate_first):
+        rows = pl.ds(pl.multiple_of(first, 32), 32)
+        gate = gate_ref[pl.ds(pl.multiple_of(gate_first, 32), 32), :].astype(F32)
+        value = (dz[rows, :] * gain[...] * gate).astype(BF)
+        for k in range(SEQ):
+            datt[k, rows, :] = value[:, 128 * k : 128 * k + 128]
+
+    def d_norm_hist(r, carry):
+        d_norm(r * 32, u_v, r * 32)
+        return carry
+
+    def d_norm_tgt(r, carry):
+        d_norm(ROWS + r * 32, tgate, r * 32)
+        return carry
+
+    target_rows = pl.ds(pl.multiple_of(HIST + s * SLOTS, SLOTS), SLOTS)
+    local_wait(u_v, LU)
+    local_wait(gain, LGA)
+    lax.fori_loop(0, 4, d_norm_hist, 0)
+    seq_send(PDH, lambda p: datt.at[p, pl.ds(0, ROWS)], da_raw.at[rows_at(s, ROWS)])
+    da_raw[rows_at(s, ROWS), :] = datt[s, pl.ds(0, ROWS), :]
 
     row512 = lax.broadcasted_iota(jnp.int32, (512, 512), 0)
     col512 = lax.broadcasted_iota(jnp.int32, (512, 512), 1)
@@ -173,20 +199,21 @@
     tq[...] = arranged[:, :128]
     for k in range(SEQ):
         tgate[:, 128 * k : 128 * k + 128] = arranged[64 * k : 64 * k + 64, 128:]
-    target_rows = pl.ds(pl.multiple_of(HIST + s * SLOTS, SLOTS), SLOTS)
     seq_send(PTQ, lambda p: tq.at[rows_at(p, SLOTS)], qraw.at[target_rows])
     qraw[target_rows, :] = tq[rows_at(s, SLOTS), :]
 
-    def group_send(phase, src, dst):
+    lax.fori_loop(0, 2, d_norm_tgt, 0)
+    seq_send(PDT, lambda p: datt.at[p, pl.ds(ROWS, SLOTS)], da_raw.at[target_rows])
+    da_raw[target_rows, :] = datt[s, pl.ds(ROWS, SLOTS), :]
+    cot_all[mine] = cot[...]
+
+    def group_send(phase, rows):
         for d in range(1, 2 * NY):
             r = lax.rem(mine + d, 2 * NY)
-            ry, rc = lax.div(r, 2), lax.rem(r, 2)
-            send(src(ry, rc), dst, phase, {"dp": ry * NZ + z, "seq": s - core + rc})
-
-    group_send(PCO, lambda ry, rc: cot.at[:, rows_at(rc, 512)], cot_all.at[mine])
-    cot_all[mine] = cot[:, rows_at(core, 512)]
-    local_wait(u_v, LU)
-    local_wait(gain, LGA)
+            send(
+                gated_p.at[rows, rows_at(r, 128)], gated_all.at[mine, rows], phase,
+                {"dp": lax.div(r, 2) * NZ + z, "seq": s - core + lax.rem(r, 2)},
+            )
 
     for buf in (kraw, qraw, vraw):
         local_wait(buf.at[pl.ds(0, ROWS)], LIN)
@@ -237,6 +264,31 @@
     stack_heads(vraw, vst)
     for i in range(4):
         attend(i)
+
+    ones = jnp.ones((128, 128), BF)
+    stat_row = lax.broadcasted_iota(jnp.int32, (16, 128), 0)
+
+    def two(value):
+        high = value.astype(BF)
+        return high, (value - high.astype(F32)).astype(BF)
+
+    def stats(i, base):
+        rows = slice(TILE * i, TILE * i + TILE)
+        att, dn = o_h[rows, :], da_raw[rows, :]
+        centred = att.astype(F32) - dot(att, ones) * (1.0 / 128.0)
+        parts = [(0, att), (2, dn)]
+        parts += [(1, part) for part in two(centred * centred)]
+        parts += [(3, part) for part in two(centred * dn.astype(F32))]
+        total = dot_nt(one_hot(stat_row == base + parts[0][0]), parts[0][1])
+        for q, part in parts[1:]:
+            total = total + dot_nt(one_hot(stat_row == base + q), part)
+        return total[:8, :]
+
+    got(da_raw.at[pl.ds(0, 896)], PDH)
+    st_hs[:, :TILE] = stats(0, 0) + stats(2, 4)
+    st_hs[:, TILE:] = stats(1, 0) + stats(3, 4)
+    seq_send(PSH, lambda p: st_hs, st_h.at[s])
+    st_h[s] = st_hs[...]
     seq_send(PAH, lambda p: o_h.at[rows_at(p, ROWS)], att_r.at[s, pl.ds(0, ROWS)])
     att_r[s, pl.ds(0, ROWS), :] = o_h[rows_at(s, ROWS), :]
 
@@ -246,12 +298,85 @@
         qs[rows, :] = (qraw[rows, :].astype(F32) * 0.0625).astype(BF)
         scores(i)
         attend(i)
+    got(da_raw.at[pl.ds(HIST, 448)], PDT)
+    st_ts[...] = stats(4, 0) + stats(5, 4)
+    seq_send(PST, lambda p: st_ts, st_t.at[s])
+    st_t[s] = st_ts[...]
     seq_send(
         PAT,
         lambda p: o_h.at[pl.ds(pl.multiple_of(HIST + p * SLOTS, SLOTS), SLOTS)],
         att_r.at[s, pl.ds(ROWS, SLOTS)],
     )
     att_r[s, pl.ds(ROWS, SLOTS), :] = o_h[target_rows, :]
+
+    def row_terms(received):
+        blocks = [received[k] for k in range(SEQ)]
+        total = blocks[0]
+        for block in blocks[1:]:
+            total = total + block
+        terms = []
+        for base in (0, 4):
+            mean = total[base : base + 1] * (1.0 / D)
+            squares, product = total[base + 1 : base + 2], total[base + 3 : base + 4]
+            for block in blocks:
+                shift = block[base : base + 1] * (1.0 / 128.0) - mean
+                squares = squares + 128.0 * shift * shift
+                product = product + block[base + 2 : base + 3] * shift
+            inverse = lax.rsqrt(squares * (1.0 / D) + 1e-05)
+            offset = inverse * total[base + 2 : base + 3] * (1.0 / D)
+            slope = inverse * inverse * (inverse * product * (1.0 / D))
+            zero = jnp.zeros_like(mean)
+            terms.append(jnp.concatenate([inverse, offset, slope, mean, zero, zero, zero, zero], axis=0))
+        return terms
+
+    spread4 = jnp.where(
+        (lax.broadcasted_iota(jnp.int32, (8, 512), 1) >> 7) == lax.broadcasted_iota(jnp.int32, (8, 512), 0), 1.0, 0.0
+    )
+
+    def d_attended(i, terms):
+        rows = slice(TILE * i, TILE * i + TILE)
+        wide = lax.dot_general(
+            terms, spread4, (((0,), (0,)), ((), ())), precision=lax.Precision.HIGHEST, preferred_element_type=F32
+        )
+        value = (
+            wide[:, :128] * da_raw[rows, :].astype(F32)
+            - wide[:, 128:256]
+            - wide[:, 256:384] * (o_h[rows, :].astype(F32) - wide[:, 384:])
+        )
+        if i < 4:
+            value = jnp.where(tile_row < length - TILE * i, value, 0.0)
+        da[rows, :] = value.astype(BF)
+
+    def backward(i):
+        rows = slice(TILE * i, TILE * i + TILE)
+        count = min(i, 3) + 1
+        for j in range(count):
+            cols = slice(WIDE * j, WIDE * j + WIDE)
+            d_weight = dot_nt(da[rows, :], vst[cols, :])
+            dsc[rows, cols] = (d_weight * gst[rows, cols].astype(F32)).astype(BF)
+        return (dot(dsc[rows, : WIDE * count], kst[: WIDE * count, :]) * 0.125).astype(BF)
+
+    def grads_send(phase, buf, base):
+        place = dqkvu_out.at[:, pl.ds(pl.multiple_of(base + s * 128, 128), 128)]
+        seq_send(phase, lambda p: buf.at[rows_at(p, ROWS)], place)
+        local(buf.at[rows_at(s, ROWS)], place, LGR)
+
+    got(st_h.at[pl.ds(0, SEQ - 1)], PSH)
+    lower, upper = row_terms(st_h)
+    for i in range(4):
+        d_attended(i, (lower, upper)[i // 2][:, TILE * (i % 2) : TILE * (i % 2) + TILE])
+    for i in range(4):
+        gq[TILE * i : TILE * i + TILE, :] = backward(i)
+    grads_send(PGQ, gq, 2 * D)
+
+    row256 = lax.broadcasted_iota(jnp.int32, (TILE, TILE), 0)
+    col256 = lax.broadcasted_iota(jnp.int32, (TILE, TILE), 1)
+    perm_core = one_hot(row256 == ((col256 & 127) >> 2) * 8 + (col256 >> 7) * 4 + (col256 & 3))
+
+    def reorder(rows):
+        for k in range(NY):
+            cols = slice(TILE * k, TILE * k + TILE)
+            gated_p[rows, cols] = dot(gated[rows, cols], perm_core).astype(BF)
 
     def norm(first, gate_ref, gate_first, du_ref):
         rows = pl.ds(pl.multiple_of(first, 32), 32)
@@ -264,15 +389,6 @@
         gated[rows, :] = (normed * gain[...] * gate).astype(BF)
         scaled = dz[rows, :] * gain[...]
         du_ref[gate_rows, :] = (scaled * normed).astype(BF)
-        d_norm = scaled * gate
-        d_att = inverse * (
-            d_norm
-            - jnp.mean(d_norm, axis=1, keepdims=True)
-            - normed * jnp.mean(d_norm * normed, axis=1, keepdims=True)
-        )
-        d_att = d_att.astype(BF)
-        for k in range(SEQ):
-            datt[k, rows, :] = d_att[:, 128 * k : 128 * k + 128]
 
     def norm_hist(r, carry):
         norm(r * 32, u_v, r * 32, du_h)
@@ -284,25 +400,61 @@
 
     got(att_r.at[pl.ds(0, 7), pl.ds(0, ROWS)], PAH)
     lax.fori_loop(0, 4, norm_hist, 0)
-    seq_send(PDH, lambda p: datt.at[p, pl.ds(0, ROWS)], da_raw.at[rows_at(s, ROWS)])
-    da_raw[rows_at(s, ROWS), :] = datt[s, pl.ds(0, ROWS), :]
     local(du_h, dqkvu_out.at[:, pl.ds(0, D)], LDU)
     hist_rows = pl.ds(0, ROWS)
     slot_rows = pl.ds(ROWS, SLOTS)
-    group_send(PGA, lambda ry, rc: gated.at[hist_rows, rows_at(ry, 256)], gated_all.at[mine, hist_rows])
+    reorder(slice(0, ROWS))
+    group_send(PGA, hist_rows)
 
     got(att_r.at[pl.ds(0, 7), pl.ds(ROWS, SLOTS)], PAT)
     lax.fori_loop(0, 2, norm_tgt, 0)
-    seq_send(PDT, lambda p: datt.at[p, pl.ds(ROWS, SLOTS)], da_raw.at[target_rows])
-    da_raw[target_rows, :] = datt[s, pl.ds(ROWS, SLOTS), :]
+    reorder(slice(ROWS, ROWS + SLOTS))
+    group_send(PGB, slot_rows)
+    gated_all[mine] = gated_p[:, rows_at(mine, 128)]
 
     gate_stack = jnp.concatenate([dgt[:, 128 * k : 128 * k + 128] for k in range(SEQ)], axis=0)
     zg[...] = dot(perm_back, gate_stack).astype(BF)
     dp_send(PGT, zg, rg)
     rg[rows_at(g, 16), :] = zg[rows_at(g, 16), :]
 
-    group_send(PGB, lambda ry, rc: gated.at[slot_rows, rows_at(ry, 256)], gated_all.at[mine, slot_rows])
-    gated_all[mine] = gated[:, rows_at(y, 256)]
+    got(cot_all.at[pl.ds(0, NY - 1)], PCO)
+    for d in range(1, NY):
+        place = cot_all.at[2 * lax.rem(y + d, NY) + core]
+        send(place, place, PCF, {"seq": other})
+
+    got(st_t.at[pl.ds(0, SEQ - 1)], PST)
+    for i, terms in enumerate(row_terms(st_t)):
+        d_attended(4 + i, terms)
+    for i in range(4, 6):
+        dqt[TILE * (i - 4) : TILE * (i - 3), :] = backward(i)
+    seq_send(PQS, lambda p: dqt.at[rows_at(p, SLOTS)], yq.at[rows_at(s, SLOTS)])
+    yq[rows_at(s, SLOTS), :] = dqt[rows_at(s, SLOTS), :]
+
+    def key_sum(left, right, j):
+        both = dot_tn(left[TILE * j : ALL, WIDE * j : WIDE * j + WIDE], right[TILE * j : ALL, :])
+        return jnp.where(lane < 64, both[:TILE, :], both[TILE:, :])
+
+    for j in range(4):
+        gk[TILE * j : TILE * j + TILE, :] = (key_sum(dsc, qs, j) * 2.0).astype(BF)
+    grads_send(PGK, gk, 3 * D)
+    for j in range(4):
+        gv[TILE * j : TILE * j + TILE, :] = key_sum(wst, da, j).astype(BF)
+    grads_send(PGV, gv, D)
+
+    got(cot_all.at[pl.ds(0, NY)], PCF)
+    got(gated_all.at[pl.ds(0, 7), hist_rows], PGA)
+    got(gated_all.at[pl.ds(0, 7), slot_rows], PGB)
+    y_own[...] = dot_tn(gated_all[...].reshape(8 * 192, 128), cot_all[...].reshape(8 * 192, D))
+    for d in range(1, NZ):
+        zp = lax.rem(z + d, NZ)
+        z_send[zp] = y_own[rows_at(zp, 16), :].astype(BF)
+        send(z_send.at[zp], z_recv.at[z], PZ, {"dp": y * NZ + zp})
+
+    got(yq.at[pl.ds(0, 448)], PQS)
+    zq[...] = dot(perm_back, yq[...]).astype(BF)
+    dp_send(PQD, zq, rq)
+    rq[rows_at(g, 16), :] = zq[rows_at(g, 16), :]
+
     outs[...] = dot(gated[:ROWS, :], w_v[...]).astype(BF)
     local(outs, ho_out, LHO)
     rows32[...] = dot(gated[ROWS:, :], w_v[...])
@@ -310,61 +462,17 @@
         to_v[h] = rows32[2 * h : 2 * h + 2, :].astype(BF)
     local(to_v, to_out, LTO)
 
-    def backward(i):
-        rows = slice(TILE * i, TILE * i + TILE)
-        count = min(i, 3) + 1
-        for j in range(count):
-            cols = slice(WIDE * j, WIDE * j + WIDE)
-            d_weight = dot_nt(da[rows, :], vst[cols, :])
-            dsc[rows, cols] = (d_weight * gst[rows, cols].astype(F32)).astype(BF)
-        return (dot(dsc[rows, : WIDE * count], kst[: WIDE * count, :]) * 0.125).astype(BF)
-
-    got(da_raw.at[pl.ds(HIST, 448)], PDT)
-    da[HIST:ALL, :] = da_raw[HIST:ALL, :]
-    for i in range(4, 6):
-        dqt[TILE * (i - 4) : TILE * (i - 3), :] = backward(i)
-    seq_send(PQS, lambda p: dqt.at[rows_at(p, SLOTS)], yq.at[rows_at(s, SLOTS)])
-    yq[rows_at(s, SLOTS), :] = dqt[rows_at(s, SLOTS), :]
-
-    got(da_raw.at[pl.ds(0, 896)], PDH)
-    for i in range(4):
-        rows = slice(TILE * i, TILE * i + TILE)
-        da[rows, :] = jnp.where(tile_row < length - TILE * i, da_raw[rows, :].astype(F32), 0.0).astype(BF)
-    for i in range(4):
-        gq[TILE * i : TILE * i + TILE, :] = backward(i)
-
-    def grads_send(phase, buf, base):
-        place = dqkvu_out.at[:, pl.ds(pl.multiple_of(base + s * 128, 128), 128)]
-        seq_send(phase, lambda p: buf.at[rows_at(p, ROWS)], place)
-        local(buf.at[rows_at(s, ROWS)], place, LGR)
-
-    grads_send(PGQ, gq, 2 * D)
-
-    def key_sum(left, right, j):
-        both = dot_tn(left[TILE * j : ALL, WIDE * j : WIDE * j + WIDE], right[TILE * j : ALL, :])
-        return jnp.where(lane < 64, both[:TILE, :], both[TILE:, :])
-
-    for j in range(4):
-        gk[TILE * j : TILE * j + TILE, :] = (key_sum(dsc, qs, j) * 2.0).astype(BF)
-    grads_send(PGK, gk, 3 * D)
-    for j in range(4):
-        gv[TILE * j : TILE * j + TILE, :] = key_sum(wst, da, j).astype(BF)
-    grads_send(PGV, gv, D)
-
-    got(yq.at[pl.ds(0, 448)], PQS)
-    zq[...] = dot(perm_back, yq[...]).astype(BF)
-    dp_send(PQD, zq, rq)
-    rq[rows_at(g, 16), :] = zq[rows_at(g, 16), :]
-
-    got(cot_all.at[pl.ds(0, 7)], PCO)
-    got(gated_all.at[pl.ds(0, 7), hist_rows], PGA)
-    got(gated_all.at[pl.ds(0, 7), slot_rows], PGB)
-    y_own[...] = dot_tn(gated_all[...].reshape(8 * 192, 256), cot_all[...].reshape(8 * 192, 512))
+    got(z_recv.at[pl.ds(0, NZ - 1)], PZ)
+    total = y_own[rows_at(z, 16), :]
     for d in range(1, NZ):
-        zp = lax.rem(z + d, NZ)
-        z_send[zp] = y_own[rows_at(zp, 32), :].astype(BF)
-        send(z_send.at[zp], z_recv.at[z], PZ, {"dp": y * NZ + zp})
-    z_own[...] = y_own[rows_at(z, 32), :]
+        total = total + z_recv[lax.rem(z + d, NZ)].astype(F32)
+    for q in range(4):
+        rows = total[4 * q : 4 * q + 4, :]
+        x_send[q] = jnp.concatenate([rows[:, :512], rows[:, 512:]], axis=0)
+    for d in range(1, 4):
+        xp = lax.rem(x + d, 4)
+        send(x_send.at[xp], x_recv.at[x], PX, {"seq": 2 * xp + core})
+    x_recv[x] = x_send[x]
 
     got(rg.at[pl.ds(0, 496)], PGT)
     got(rq.at[pl.ds(0, 496)], PQD)
@@ -375,17 +483,9 @@
         di[:, D + 128 * k : D + 128 * k + 128] = d_items[64 * k : 64 * k + 64, 128:]
     local(di, di_out, LDI)
 
-    got(z_recv.at[pl.ds(0, NZ - 1)], PZ)
-    total = z_own[...]
-    for d in range(1, NZ):
-        total = total + z_recv[lax.rem(z + d, NZ)].astype(F32)
-    x_send[...] = total
-    seq_send(PX, lambda p: x_send.at[rows_at(lax.div(p, 2), 8)], x_recv.at[s])
-    x_recv[s] = x_send[rows_at(lax.div(s, 2), 8), :]
-    got(x_recv.at[pl.ds(0, SEQ - 1)], PX)
-    halves = [x_recv[c] + x_recv[2 + c] + x_recv[4 + c] + x_recv[6 + c] for c in range(2)]
-    full = jnp.concatenate(halves, axis=1) * (32768.0 ** -0.5)
-    dw[...] = jnp.where(core == 0, full[:4, :], full[4:, :])
+    got(x_recv.at[pl.ds(0, 3)], PX)
+    full = (x_recv[0] + x_recv[1] + x_recv[2] + x_recv[3]) * (32768.0 ** -0.5)
+    dw[...] = jnp.concatenate([full[:4, :], full[4:, :]], axis=1)
     local(dw, dw_out, LDW)
 
     for phase, buf in ((PGQ, gq), (PGK, gk), (PGV, gv)):
@@ -398,11 +498,14 @@
         sent(buf.at[pl.ds(0, 448)], phase)
     for phase, buf in ((PT, tsend), (PGT, zg), (PQD, zq)):
         sent(buf.at[pl.ds(0, 496)], phase)
-    sent(cot_all.at[pl.ds(0, 7)], PCO)
+    sent(cot_all.at[pl.ds(0, NY - 1)], PCO)
+    sent(cot_all.at[pl.ds(0, NY)], PCF)
+    sent(st_h.at[pl.ds(0, SEQ - 1)], PSH)
+    sent(st_t.at[pl.ds(0, SEQ - 1)], PST)
     sent(gated_all.at[pl.ds(0, 7), hist_rows], PGA)
     sent(gated_all.at[pl.ds(0, 7), slot_rows], PGB)
     sent(z_send.at[pl.ds(0, NZ - 1)], PZ)
-    sent(x_recv.at[pl.ds(0, SEQ - 1)], PX)
+    sent(x_recv.at[pl.ds(0, 3)], PX)
     local_wait(du_h, LDU)
     local_wait(outs, LHO)
     local_wait(to_v, LTO)
@@ -437,9 +540,11 @@
         vm(ROWS + SLOTS, D), vm(ROWS, D), vm(ROWS, D), vm(SLOTS, D),
         vm(512, 128), vm(512, 128), vm(512, 128), vm(512, 128), vm(512, 128), vm(512, 128),
         vm(HIST, 128), vm(HIST, 128), vm(HIST, 128), vm(SLOTS, 2 * D),
-        vm(8, ROWS + SLOTS, 512), vm(8, ROWS + SLOTS, 256), vm(256, 512, dtype=F32),
-        vm(NZ, 32, 512), vm(32, 512, dtype=F32), vm(NZ, 32, 512),
-        vm(32, 512, dtype=F32), vm(SEQ, 8, 512, dtype=F32), vm(4, D, dtype=F32),
+        vm(8, 512, dtype=F32), vm(8, TILE, dtype=F32),
+        vm(SEQ, 8, 512, dtype=F32), vm(SEQ, 8, TILE, dtype=F32),
+        vm(ROWS + SLOTS, D), vm(8, ROWS + SLOTS, D), vm(8, ROWS + SLOTS, 128),
+        vm(128, D, dtype=F32), vm(NZ, 16, D), vm(NZ, 16, D),
+        vm(4, 8, 512, dtype=F32), vm(4, 8, 512, dtype=F32), vm(4, D, dtype=F32),
         pltpu.SemaphoreType.DMA((NPH,)),
         pltpu.SemaphoreType.DMA((NPH,)),
         pltpu.SemaphoreType.DMA((NLOC,)),

time: 67.6 us -> 61.1 us (0.904)
  Pallas kernels: 66.1 us -> 59.6 us
    pallas_call x1, Pallas kernels: 64.8 us -> 58.3 us  [shards(): pl.pallas_call(kernel, out_shape=(pltpu.VMEM((ROWS, D), BF), pltpu.VMEM((...]
where the time goes in v3:
time: 61.1 us; the launch traced here: 61 us
  Pallas kernels  59.6 us (98%)
  between operations  1.45 us (2%)
    pallas_call x1, Pallas kernels, shards(): pl.pallas_call(kernel, out_shape=(pltpu.VMEM((ROWS, D), BF), pltpu.VMEM((...  58.3 us
    pallas_call x1, Pallas kernels, shards(): pl.pallas_call(deliver, out_shape=tuple((jax.ShapeDtypeStruct(r.shape, r....  1.25 us

profile of v3, /device:TPU:1, one launch (start us, length us, event | category | flops | bytes accessed | tf_op | source)
XLA Modules:
  0.0 61.0 jit_solution(13453571562943781026)
XLA Ops:
  1.3 58.3 %shard_map.128 = (bf16[128,1024]{1,0:T(8,128)(2,1)S(1)}, bf16[32,2,1024]{2,1,0:T(2,128)(2,1)S(1)}, bf16[128,4096]{1,0:T(8,128)(2,1)S(1)}, bf16[64,2048]{1,0:T(8,128)(2,1)S(1)}, f32[4,1024]{1,0:T(4,128)S(1)}) custom-call(s32[2,32]{1,0:T(2,128)} %bitcast.18, s32[1,32]{1,0:T(1,128)} %bitcast.19, s32[1]{0:T(128)S(6)} %copy.14.length_ref, ...), custom_call_target="tpu_custom_call" | custom-call | tf_op jit(solution)/shard_map/pallas_call | solution.py:557
  59.6 1.3 %shard_map.129 = (bf16[128,1024]{1,0:T(8,128)(2,1)}, bf16[32,2,1024]{2,1,0:T(2,128)(2,1)}, bf16[128,4096]{1,0:T(8,128)(2,1)}, bf16[64,2048]{1,0:T(8,128)(2,1)}, f32[4,1024]{1,0:T(4,128)}) custom-call(bf16[128,1024]{1,0:T(8,128)(2,1)S(1)} %get-tuple-element.15.ho, bf16[32,2,1024]{2,1,0:T(2,128)(2,1)S(1)} %get-tuple-element.16.to, ...), custom_call_target="tpu_custom_call" | custom-call | tf_op jit(solution)/shard_map/pallas_call | solution.py:575

commit v4 on v3

--- a/solution.py
+++ b/solution.py
@@ -298,15 +298,15 @@
         qs[rows, :] = (qraw[rows, :].astype(F32) * 0.0625).astype(BF)
         scores(i)
         attend(i)
-    got(da_raw.at[pl.ds(HIST, 448)], PDT)
-    st_ts[...] = stats(4, 0) + stats(5, 4)
-    seq_send(PST, lambda p: st_ts, st_t.at[s])
-    st_t[s] = st_ts[...]
     seq_send(
         PAT,
         lambda p: o_h.at[pl.ds(pl.multiple_of(HIST + p * SLOTS, SLOTS), SLOTS)],
         att_r.at[s, pl.ds(ROWS, SLOTS)],
     )
+    got(da_raw.at[pl.ds(HIST, 448)], PDT)
+    st_ts[...] = stats(4, 0) + stats(5, 4)
+    seq_send(PST, lambda p: st_ts, st_t.at[s])
+    st_t[s] = st_ts[...]
     att_r[s, pl.ds(ROWS, SLOTS), :] = o_h[target_rows, :]
 
     def row_terms(received):
@@ -325,19 +325,19 @@
             inverse = lax.rsqrt(squares * (1.0 / D) + 1e-05)
             offset = inverse * total[base + 2 : base + 3] * (1.0 / D)
             slope = inverse * inverse * (inverse * product * (1.0 / D))
-            zero = jnp.zeros_like(mean)
-            terms.append(jnp.concatenate([inverse, offset, slope, mean, zero, zero, zero, zero], axis=0))
+            exact = jnp.concatenate([inverse, offset, slope, mean], axis=0)
+            high = exact.astype(BF).astype(F32)
+            middle = (exact - high).astype(BF).astype(F32)
+            low = exact - high - middle
+            terms.append(jnp.concatenate([high, middle, low, jnp.zeros_like(low)], axis=0).astype(BF))
         return terms
 
-    spread4 = jnp.where(
-        (lax.broadcasted_iota(jnp.int32, (8, 512), 1) >> 7) == lax.broadcasted_iota(jnp.int32, (8, 512), 0), 1.0, 0.0
-    )
+    spread_lane = lax.broadcasted_iota(jnp.int32, (16, 512), 1) >> 7
+    spread4 = one_hot(spread_lane == (lax.broadcasted_iota(jnp.int32, (16, 512), 0) & 3))
 
     def d_attended(i, terms):
         rows = slice(TILE * i, TILE * i + TILE)
-        wide = lax.dot_general(
-            terms, spread4, (((0,), (0,)), ((), ())), precision=lax.Precision.HIGHEST, preferred_element_type=F32
-        )
+        wide = dot_tn(terms, spread4)
         value = (
             wide[:, :128] * da_raw[rows, :].astype(F32)
             - wide[:, 128:256]
@@ -430,9 +430,19 @@
     seq_send(PQS, lambda p: dqt.at[rows_at(p, SLOTS)], yq.at[rows_at(s, SLOTS)])
     yq[rows_at(s, SLOTS), :] = dqt[rows_at(s, SLOTS), :]
 
+    got(cot_all.at[pl.ds(0, NY)], PCF)
+    got(gated_all.at[pl.ds(0, 7), hist_rows], PGA)
+    y_own[...] = dot_tn(gated_all[:, :ROWS, :].reshape(8 * ROWS, 128), cot_all[:, :ROWS, :].reshape(8 * ROWS, D))
+    got(gated_all.at[pl.ds(0, 7), slot_rows], PGB)
+    y_own[...] += dot_tn(gated_all[:, ROWS:, :].reshape(8 * SLOTS, 128), cot_all[:, ROWS:, :].reshape(8 * SLOTS, D))
+    for d in range(1, NZ):
+        zp = lax.rem(z + d, NZ)
+        z_send[zp] = y_own[rows_at(zp, 16), :].astype(BF)
+        send(z_send.at[zp], z_recv.at[z], PZ, {"dp": y * NZ + zp})
+
     def key_sum(left, right, j):
-        both = dot_tn(left[TILE * j : ALL, WIDE * j : WIDE * j + WIDE], right[TILE * j : ALL, :])
-        return jnp.where(lane < 64, both[:TILE, :], both[TILE:, :])
+        both = dot_tn(right[TILE * j : ALL, :], left[TILE * j : ALL, WIDE * j : WIDE * j + WIDE])
+        return jnp.concatenate([both[:64, :TILE], both[64:, TILE:]], axis=0).T
 
     for j in range(4):
         gk[TILE * j : TILE * j + TILE, :] = (key_sum(dsc, qs, j) * 2.0).astype(BF)
@@ -440,15 +450,6 @@
     for j in range(4):
         gv[TILE * j : TILE * j + TILE, :] = key_sum(wst, da, j).astype(BF)
     grads_send(PGV, gv, D)
-
-    got(cot_all.at[pl.ds(0, NY)], PCF)
-    got(gated_all.at[pl.ds(0, 7), hist_rows], PGA)
-    got(gated_all.at[pl.ds(0, 7), slot_rows], PGB)
-    y_own[...] = dot_tn(gated_all[...].reshape(8 * 192, 128), cot_all[...].reshape(8 * 192, D))
-    for d in range(1, NZ):
-        zp = lax.rem(z + d, NZ)
-        z_send[zp] = y_own[rows_at(zp, 16), :].astype(BF)
-        send(z_send.at[zp], z_recv.at[z], PZ, {"dp": y * NZ + zp})
 
     got(yq.at[pl.ds(0, 448)], PQS)
     zq[...] = dot(perm_back, yq[...]).astype(BF)

time: 61.1 us -> 59.2 us (0.969)
  Pallas kernels: 59.6 us -> 57.7 us
    pallas_call x1, Pallas kernels: 58.3 us -> 56.4 us  [shards(): pl.pallas_call(kernel, out_shape=(pltpu.VMEM((ROWS, D), BF), pltpu.VMEM((...]
where the time goes in v4:
time: 59.2 us; the launch traced here: 59.1 us
  Pallas kernels  57.7 us (97%)
  between operations  1.45 us (2%)
    pallas_call x1, Pallas kernels, shards(): pl.pallas_call(kernel, out_shape=(pltpu.VMEM((ROWS, D), BF), pltpu.VMEM((...  56.4 us
    pallas_call x1, Pallas kernels, shards(): pl.pallas_call(deliver, out_shape=tuple((jax.ShapeDtypeStruct(r.shape, r....  1.25 us

profile of v4, /device:TPU:1, one launch (start us, length us, event | category | flops | bytes accessed | tf_op | source)
XLA Modules:
  0.0 59.1 jit_solution(5208978523635735488)
XLA Ops:
  1.3 56.4 %shard_map.128 = (bf16[128,1024]{1,0:T(8,128)(2,1)S(1)}, bf16[32,2,1024]{2,1,0:T(2,128)(2,1)S(1)}, bf16[128,4096]{1,0:T(8,128)(2,1)S(1)}, bf16[64,2048]{1,0:T(8,128)(2,1)S(1)}, f32[4,1024]{1,0:T(4,128)S(1)}) custom-call(s32[2,32]{1,0:T(2,128)} %bitcast.18, s32[1,32]{1,0:T(1,128)} %bitcast.19, s32[1]{0:T(128)S(6)} %copy.14.length_ref, ...), custom_call_target="tpu_custom_call" | custom-call | tf_op jit(solution)/shard_map/pallas_call | solution.py:558
  57.7 1.3 %shard_map.129 = (bf16[128,1024]{1,0:T(8,128)(2,1)}, bf16[32,2,1024]{2,1,0:T(2,128)(2,1)}, bf16[128,4096]{1,0:T(8,128)(2,1)}, bf16[64,2048]{1,0:T(8,128)(2,1)}, f32[4,1024]{1,0:T(4,128)}) custom-call(bf16[128,1024]{1,0:T(8,128)(2,1)S(1)} %get-tuple-element.15.ho, bf16[32,2,1024]{2,1,0:T(2,128)(2,1)S(1)} %get-tuple-element.16.to, ...), custom_call_target="tpu_custom_call" | custom-call | tf_op jit(solution)/shard_map/pallas_call | solution.py:576

commit v5 on v4

--- a/solution.py
+++ b/solution.py
@@ -368,6 +368,11 @@
     for i in range(4):
         gq[TILE * i : TILE * i + TILE, :] = backward(i)
     grads_send(PGQ, gq, 2 * D)
+    got(cot_all.at[pl.ds(0, NY - 1)], PCO)
+    for d in range(1, NY):
+        place = cot_all.at[2 * lax.rem(y + d, NY) + core]
+        send(place, place, PCF, {"seq": other})
+
 
     row256 = lax.broadcasted_iota(jnp.int32, (TILE, TILE), 0)
     col256 = lax.broadcasted_iota(jnp.int32, (TILE, TILE), 1)
@@ -416,11 +421,6 @@
     zg[...] = dot(perm_back, gate_stack).astype(BF)
     dp_send(PGT, zg, rg)
     rg[rows_at(g, 16), :] = zg[rows_at(g, 16), :]
-
-    got(cot_all.at[pl.ds(0, NY - 1)], PCO)
-    for d in range(1, NY):
-        place = cot_all.at[2 * lax.rem(y + d, NY) + core]
-        send(place, place, PCF, {"seq": other})
 
     got(st_t.at[pl.ds(0, SEQ - 1)], PST)
     for i, terms in enumerate(row_terms(st_t)):

time: 59.2 us -> 59.2 us (level)
  no operation moved by 1% of the time
where the time goes in v5:
time: 59.2 us; the launch traced here: 59.1 us
  Pallas kernels  57.7 us (97%)
  between operations  1.45 us (2%)
    pallas_call x1, Pallas kernels, shards(): pl.pallas_call(kernel, out_shape=(pltpu.VMEM((ROWS, D), BF), pltpu.VMEM((...  56.4 us
    pallas_call x1, Pallas kernels, shards(): pl.pallas_call(deliver, out_shape=tuple((jax.ShapeDtypeStruct(r.shape, r....  1.25 us

profile of v5, /device:TPU:1, one launch (start us, length us, event | category | flops | bytes accessed | tf_op | source)
XLA Modules:
  0.0 59.1 jit_solution(14771781451528062291)
XLA Ops:
  1.3 56.4 %shard_map.128 = (bf16[128,1024]{1,0:T(8,128)(2,1)S(1)}, bf16[32,2,1024]{2,1,0:T(2,128)(2,1)S(1)}, bf16[128,4096]{1,0:T(8,128)(2,1)S(1)}, bf16[64,2048]{1,0:T(8,128)(2,1)S(1)}, f32[4,1024]{1,0:T(4,128)S(1)}) custom-call(s32[2,32]{1,0:T(2,128)} %bitcast.18, s32[1,32]{1,0:T(1,128)} %bitcast.19, s32[1]{0:T(128)S(6)} %copy.14.length_ref, ...), custom_call_target="tpu_custom_call" | custom-call | tf_op jit(solution)/shard_map/pallas_call | solution.py:558
  57.7 1.3 %shard_map.129 = (bf16[128,1024]{1,0:T(8,128)(2,1)}, bf16[32,2,1024]{2,1,0:T(2,128)(2,1)}, bf16[128,4096]{1,0:T(8,128)(2,1)}, bf16[64,2048]{1,0:T(8,128)(2,1)}, f32[4,1024]{1,0:T(4,128)}) custom-call(bf16[128,1024]{1,0:T(8,128)(2,1)S(1)} %get-tuple-element.15.ho, bf16[32,2,1024]{2,1,0:T(2,128)(2,1)S(1)} %get-tuple-element.16.to, ...), custom_call_target="tpu_custom_call" | custom-call | tf_op jit(solution)/shard_map/pallas_call | solution.py:576
